TPU v7x, 256 devices: a whole 4x4x8 slice. The times are simulated.
256 devices in a mesh: seq: 64 (over x_hi, z, y), mp: 4 (over x_lo, core).
Axes of the slice: x: 4 (x_hi: 2, x_lo: 2; x = x_hi * 2 + x_lo), y: 4, z: 8, core: 2. Of those that a mesh axis runs over, the one named last changes fastest.
Arguments:
- queries: bfloat16 [16384, 1280], P('seq', 'mp'), may hold values from -77 to 77
- keys: bfloat16 [32768, 1280], P('seq', 'mp'), may hold values from -4 to 4
- values: bfloat16 [32768, 1280], P('seq', 'mp'), may hold values from -48 to 48
- out_weight: bfloat16 [1280, 1280], P('mp'), may hold values from -0.15625 to 0.15625
- grad_out: bfloat16 [16384, 1280], P('seq', 'mp'), may hold values from -24 to 24
- alignment: int32 [128, 2], P('seq'), may hold values from 0 to 256, as said below
Outputs:
- layer_output: bfloat16 [16384, 1280], P('seq', 'mp')
- query_grad: bfloat16 [16384, 1280], P('seq', 'mp')
- key_grad: bfloat16 [32768, 1280], P('seq', 'mp')
- value_grad: bfloat16 [32768, 1280], P('seq', 'mp')
Inputs may be any that keep to these rules, and one draw needn't show every extreme that they name: Row g of alignment belongs to decoder block g, held by seq index i = g // 2. With k = 4: alignment[g, 0] < alignment[g, 1], max(0, (i - 1) * k) <= alignment[g, 0] <= i * k, and min(256, (i + 1) * k + 1) <= alignment[g, 1] <= min(256, (i + 3) * k).
All inputs are finite; a program needn't handle non-finite values.
Results may differ from a plain program's by a relative error of at most 0.012.
The roundings to bfloat16 on the way count: a program that leaves them out, or rounds other values in their place, can miss the bound.
Values may be sent and summed in bfloat16 or wider, within the bound.
No kernel may reach another device: no remote copies, remote signals or barrier semaphores. Data moves between devices by JAX's collectives and lax.ppermute only.
A program may use at most 64 MiB of HBM per device.

v0:
```python
import jax
import jax.numpy as jnp
from jax import lax
from jax.sharding import PartitionSpec as P

DH = 64
BLK = 128


def passed_along(value, axis, by):
    count = lax.axis_size(axis)
    pairs = [(i, i + by) for i in range(count) if 0 <= i + by < count]
    return lax.ppermute(value, axis, pairs)


def dot_rows(first_op, second_op):
    return lax.dot_general(
        first_op, second_op, (((1,), (1,)), ((), ())), preferred_element_type=jnp.float32
    )


def dot_cols(first_op, second_op):
    return lax.dot_general(
        first_op, second_op, (((0,), (0,)), ((), ())), preferred_element_type=jnp.float32
    )


def allowed(key_blocks, ranges):
    lower_rows = jnp.repeat(ranges[:, 0], BLK)
    upper_rows = jnp.repeat(ranges[:, 1], BLK)
    return (key_blocks[None, :] >= lower_rows[:, None]) & (
        key_blocks[None, :] < upper_rows[:, None]
    )


def on_device(queries, keys, values, out_weight, grad_out, alignment):
    factor = DH ** (-0.5)
    frame_rows = keys.shape[0]
    feat_cols = queries.shape[1]
    head_count = feat_cols // DH
    frame_blocks = frame_rows // BLK
    position = lax.axis_index("seq")
    grad_attended = dot_rows(lax.all_gather(grad_out, "mp", axis=1, tiled=True), out_weight).astype(
        jnp.bfloat16
    )
    received = [passed_along((keys, values), "seq", shift_by) for shift_by in (1, -1, -2)]
    window_keys = jnp.concatenate([received[0][0], keys, received[1][0], received[2][0]], axis=0)
    window_values = jnp.concatenate(
        [received[0][1], values, received[1][1], received[2][1]], axis=0
    )
    window_blocks = (position - 1) * frame_blocks + jnp.arange(
        4 * frame_rows, dtype=jnp.int32
    ) // BLK
    permit = allowed(window_blocks, alignment)
    attended_parts, query_parts, key_parts, value_parts = ([], [], [], [])
    logsum_parts, delta_parts = ([], [])
    for head_index in range(head_count):
        columns = slice(head_index * DH, (head_index + 1) * DH)
        query_head = queries[:, columns]
        key_head = window_keys[:, columns]
        value_head = window_values[:, columns]
        grad_head = grad_attended[:, columns]
        scores = jnp.where(permit, dot_rows(query_head, key_head) * factor, -jnp.inf)
        top_score = jnp.max(scores, axis=1, keepdims=True)
        logsum = top_score + jnp.log(jnp.sum(jnp.exp(scores - top_score), axis=1, keepdims=True))
        prob_full = jnp.exp(scores - logsum)
        prob_low = prob_full.astype(jnp.bfloat16)
        attended = jnp.dot(prob_low, value_head, preferred_element_type=jnp.float32).astype(
            jnp.bfloat16
        )
        row_delta = jnp.sum(
            grad_head.astype(jnp.float32) * attended.astype(jnp.float32), axis=1, keepdims=True
        )
        dprobs = dot_rows(grad_head, value_head)
        dscores = (prob_full * (dprobs - row_delta) * factor).astype(jnp.bfloat16)
        query_parts.append(
            jnp.dot(dscores, key_head, preferred_element_type=jnp.float32).astype(jnp.bfloat16)
        )
        attended_parts.append(attended)
        logsum_parts.append(logsum[:, 0])
        delta_parts.append(row_delta[:, 0])
        key_parts.append(dot_cols(dscores, query_head))
        value_parts.append(dot_cols(prob_low, grad_head))
    attended_all = jnp.concatenate(attended_parts, axis=1)
    query_grad = jnp.concatenate(query_parts, axis=1)
    key_window = jnp.concatenate(key_parts, axis=1)
    value_window = jnp.concatenate(value_parts, axis=1)
    key_total = key_window[frame_rows : 2 * frame_rows]
    value_total = value_window[frame_rows : 2 * frame_rows]
    for shift_by, slot_index in ((-1, 0), (1, 2), (2, 3)):
        first_row = slot_index * frame_rows
        returned = passed_along(
            (
                key_window[first_row : first_row + frame_rows],
                value_window[first_row : first_row + frame_rows],
            ),
            "seq",
            shift_by,
        )
        key_total = key_total + returned[0]
        value_total = value_total + returned[1]
    partial_value = jnp.dot(attended_all, out_weight, preferred_element_type=jnp.float32)
    layer_output = lax.psum_scatter(partial_value, "mp", scatter_dimension=1, tiled=True).astype(
        jnp.bfloat16
    )
    return (
        layer_output,
        query_grad,
        key_total.astype(jnp.bfloat16),
        value_total.astype(jnp.bfloat16),
    )


def solution(mesh):
    return jax.shard_map(
        on_device,
        mesh=mesh,
        in_specs=(
            P("seq", "mp"),
            P("seq", "mp"),
            P("seq", "mp"),
            P("mp", None),
            P("seq", "mp"),
            P("seq", None),
        ),
        out_specs=(P("seq", "mp"), P("seq", "mp"), P("seq", "mp"), P("seq", "mp")),
        check_vma=False,
    )
```

profile of v0, /device:TPU:27, one launch (start us, length us, event | category | flops | bytes accessed | tf_op | source)
XLA Modules:
  0.0 156.8 jit_solution(14522387047633010126)
XLA Ops:
  7.2 3.3 %collective-permute-start = (bf16[512,320]{0,1:T(8,128)(2,1)}, bf16[512,320]{0,1:T(8,128)(2,1)}, u32[]{:S(2)}, u32[]{:S(2)}) collective-permute-start(bf16[512,320]{0,1:T(8,128)(2,1)} %param.7), channel_id=1, source_target_pairs={{0,4},{4,8},{8,12},{12,16},{16,20},{20,24},{24,28},{28,32},{32,36}... | collective-permute-start | bytes 983048 | tf_op jit(solution)/shard_map/ppermute | solution.py:13
  10.6 2.1 %collective-permute-start.1 = (bf16[512,320]{0,1:T(8,128)(2,1)}, bf16[512,320]{0,1:T(8,128)(2,1)S(1)}, u32[]{:S(2)}, u32[]{:S(2)}) collective-permute-start(bf16[512,320]{0,1:T(8,128)(2,1)} %param.7), channel_id=1, source_target_pairs={{4,0},{8,4},{12,8},{16,12},{20,16},{24,20},{28,24},{32,28},{36,32}... | collective-permute-start | bytes 983048 | tf_op jit(solution)/shard_map/ppermute | solution.py:13
  12.7 3.6 %collective-permute-start.2 = (bf16[512,320]{0,1:T(8,128)(2,1)}, bf16[512,320]{0,1:T(8,128)(2,1)S(1)}, u32[]{:S(2)}, u32[]{:S(2)}) collective-permute-start(bf16[512,320]{0,1:T(8,128)(2,1)} %param.7), channel_id=1, source_target_pairs={{8,0},{12,4},{16,8},{20,12},{24,16},{28,20},{32,24},{36,28},{40,32... | collective-permute-start | bytes 983048 | tf_op jit(solution)/shard_map/ppermute | solution.py:13
  16.2 4.0 %collective-permute-start.3 = (bf16[512,320]{0,1:T(8,128)(2,1)}, bf16[512,320]{0,1:T(8,128)(2,1)S(1)}, u32[]{:S(2)}, u32[]{:S(2)}) collective-permute-start(bf16[512,320]{0,1:T(8,128)(2,1)} %param.8), channel_id=1, source_target_pairs={{0,4},{4,8},{8,12},{12,16},{16,20},{20,24},{24,28},{28,32},{32,36}... | collective-permute-start | bytes 983048 | tf_op jit(solution)/shard_map/ppermute | solution.py:13
  20.3 1.9 %collective-permute-start.4 = (bf16[512,320]{0,1:T(8,128)(2,1)}, bf16[512,320]{0,1:T(8,128)(2,1)S(1)}, u32[]{:S(2)}, u32[]{:S(2)}) collective-permute-start(bf16[512,320]{0,1:T(8,128)(2,1)} %param.8), channel_id=1, source_target_pairs={{4,0},{8,4},{12,8},{16,12},{20,16},{24,20},{28,24},{32,28},{36,32}... | collective-permute-start | bytes 983048 | tf_op jit(solution)/shard_map/ppermute | solution.py:13
  23.2 8.8 %all_gather.3 = bf16[256,1280]{0,1:T(8,128)(2,1)S(1)} all-gather(bf16[256,320]{0,1:T(8,128)(2,1)} %param.10), channel_id=1, replica_groups=mesh['seq'=64,'mp'=4] {'mp'}, dimensions={1}, use_global_device_ids=true | all-gather | bytes 819200 | tf_op jit(solution)/shard_map/all_gather | solution.py:43
  32.4 1.9 %collective-permute-start.5 = (bf16[512,320]{0,1:T(8,128)(2,1)S(1)}, bf16[512,320]{0,1:T(8,128)(2,1)S(1)}, u32[]{:S(2)}, u32[]{:S(2)}) collective-permute-start(bf16[512,320]{0,1:T(8,128)(2,1)S(1)} %copy-done.9), channel_id=1, source_target_pairs={{8,0},{12,4},{16,8},{20,12},{24,16},{28,20},{32,24},{36,28},{40,32... | collective-permute-start | bytes 983048 | tf_op jit(solution)/shard_map/ppermute | solution.py:13
  34.3 1.0 constant_dynamic-update-slice_fusion.7
  43.0 1.4 fusion.95
  44.4 5.7 %collective-permute-start.10 = (f32[512,320]{0,1:T(8,128)}, f32[512,320]{0,1:T(8,128)}, u32[]{:S(2)}, u32[]{:S(2)}) collective-permute-start(f32[512,320]{0,1:T(8,128)} %get-tuple-element.13), channel_id=1, source_target_pairs={{0,4},{4,8},{8,12},{12,16},{16,20},{20,24},{24,28},{28,32},{32,36}... | collective-permute-start | bytes 1966088 | tf_op jit(solution)/shard_map/ppermute | solution.py:13
  50.1 4.3 %collective-permute-start.11 = (f32[512,320]{0,1:T(8,128)}, f32[512,320]{0,1:T(8,128)}, u32[]{:S(2)}, u32[]{:S(2)}) collective-permute-start(f32[512,320]{0,1:T(8,128)} %get-tuple-element.12), channel_id=1, source_target_pairs={{0,8},{4,12},{8,16},{12,20},{16,24},{20,28},{24,32},{28,36},{32,40... | collective-permute-start | bytes 1966088 | tf_op jit(solution)/shard_map/ppermute | solution.py:13
  54.4 2.1 %collective-permute-start.9 = (f32[512,320]{0,1:T(8,128)}, f32[512,320]{0,1:T(8,128)}, u32[]{:S(2)}, u32[]{:S(2)}) collective-permute-start(f32[512,320]{0,1:T(8,128)} %get-tuple-element.11), channel_id=1, source_target_pairs={{4,0},{8,4},{12,8},{16,12},{20,16},{24,20},{28,24},{32,28},{36,32}... | collective-permute-start | bytes 1966088 | tf_op jit(solution)/shard_map/ppermute | solution.py:13
  59.8 1.3 convolution_dynamic-update-slice_fusion.9
  61.1 1.7 %fusion.23 = bf16[256,2048]{0,1:T(8,128)(2,1)} fusion(f32[256,2048]{0,1:T(8,128)S(1)} %get-tuple-element.22, f32[256]{0:T(256)S(1)} %get-tuple-element.6, f32[256]{0:T(256)S(1)} %log_add_fusion.3, bf16[2048,320]{0,1:T(8,128)(2,1)S(1)} %constant_dynamic-update-slice_fusion, bf16[256,320]{0,1:T(8,128)(2,1)S(1)} %convolution_convert_fusion), kind=kOutput, calls=%fused_computation.33 | convolution fusion | flops 69730304 | bytes 3442688 | tf_op jit(solution)/shard_map/dot_general | solution.py:17
  62.8 1.7 %fusion.22 = bf16[256,2048]{0,1:T(8,128)(2,1)} fusion(f32[256,2048]{0,1:T(8,128)S(1)} %get-tuple-element.26, f32[256]{0:T(256)S(1)} %get-tuple-element.7, f32[256]{0:T(256)S(1)} %log_add_fusion.2, bf16[2048,320]{0,1:T(8,128)(2,1)S(1)} %constant_dynamic-update-slice_fusion, bf16[256,320]{0,1:T(8,128)(2,1)S(1)} %convolution_convert_fusion), kind=kOutput, calls=%fused_computation.32 | convolution fusion | flops 69730304 | bytes 3442688 | tf_op jit(solution)/shard_map/dot_general | solution.py:17
  65.8 1.6 %fusion.102 = f32[256,1280]{0,1:T(8,128)} fusion(bf16[256,320]{0,1:T(8,128)(2,1)S(1)} %get-tuple-element.35, bf16[320,1280]{1,0:T(8,128)(2,1)S(1)} %copy-done), kind=kOutput, calls=%fused_computation.167 | convolution fusion | flops 209715200 | bytes 2293760 | tf_op jit(solution)/shard_map/dot_general | solution.py:102
  67.5 2.5 %convolution_dynamic-update-slice_fusion.8 = f32[2048,320]{0,1:T(8,128)} fusion(f32[2048,320]{0,1:T(8,128)} %convolution_dynamic-update-slice_fusion.9, bf16[256,2048]{0,1:T(8,128)(2,1)} %fusion.23, bf16[256,320]{0,1:T(8,128)(2,1)S(1)} %copy-done.11), kind=kOutput, calls=%fused_computation.43 | convolution fusion | flops 67108864 | bytes 1605632 | tf_op jit(solution)/shard_map/dot_general | solution.py:23
  70.0 1.3 convolution_dynamic-update-slice_fusion.7
  71.3 1.2 convolution_dynamic-update-slice_fusion.6
  72.5 1.3 convolution_dynamic-update-slice_fusion.5
  73.8 1.8 %fusion.96 = (f32[512,320]{0,1:T(8,128)S(1)}, f32[512,320]{0,1:T(8,128)S(1)}, f32[512,320]{0,1:T(8,128)S(1)}) fusion(f32[2048,320]{0,1:T(8,128)} %convolution_dynamic-update-slice_fusion.5), kind=kLoop, calls=%fused_computation.161 | loop fusion | bytes 3932160 | tf_op jit(solution)/shard_map/slice | solution.py:94
  75.6 3.0 %collective-permute-start.6 = (f32[512,320]{0,1:T(8,128)S(1)}, f32[512,320]{0,1:T(8,128)S(1)}, u32[]{:S(2)}, u32[]{:S(2)}) collective-permute-start(f32[512,320]{0,1:T(8,128)S(1)} %get-tuple-element.14), channel_id=1, source_target_pairs={{4,0},{8,4},{12,8},{16,12},{20,16},{24,20},{28,24},{32,28},{36,32}... | collective-permute-start | bytes 1966088 | tf_op jit(solution)/shard_map/ppermute | solution.py:13
  78.6 4.4 %collective-permute-start.7 = (f32[512,320]{0,1:T(8,128)S(1)}, f32[512,320]{0,1:T(8,128)S(1)}, u32[]{:S(2)}, u32[]{:S(2)}) collective-permute-start(f32[512,320]{0,1:T(8,128)S(1)} %get-tuple-element.16), channel_id=1, source_target_pairs={{0,4},{4,8},{8,12},{12,16},{16,20},{20,24},{24,28},{28,32},{32,36}... | collective-permute-start | bytes 1966088 | tf_op jit(solution)/shard_map/ppermute | solution.py:13
  83.9 3.1 %collective-permute-start.8 = (f32[512,320]{0,1:T(8,128)S(1)}, f32[512,320]{0,1:T(8,128)S(1)}, u32[]{:S(2)}, u32[]{:S(2)}) collective-permute-start(f32[512,320]{0,1:T(8,128)S(1)} %get-tuple-element.15), channel_id=1, source_target_pairs={{0,8},{4,12},{8,16},{12,20},{16,24},{20,28},{24,32},{28,36},{32,40... | collective-permute-start | bytes 1966088 | tf_op jit(solution)/shard_map/ppermute | solution.py:13
  87.7 3.1 %collective-permute-done.11 = f32[512,320]{0,1:T(8,128)} collective-permute-done((f32[512,320]{0,1:T(8,128)}, f32[512,320]{0,1:T(8,128)}, u32[]{:S(2)}, u32[]{:S(2)}) %collective-permute-start.11) | collective-permute-done | bytes 655392 | tf_op jit(solution)/shard_map/ppermute | solution.py:13
  90.7 2.6 %fusion.37 = bf16[512,320]{0,1:T(8,128)(2,1)} fusion(f32[512,320]{0,1:T(8,128)} %collective-permute-done.11, f32[512,320]{0,1:T(8,128)} %collective-permute-done.10, f32[512,320]{0,1:T(8,128)} %collective-permute-done.9, f32[2048,320]{0,1:T(8,128)} %copy-done.5), kind=kLoop, calls=%fused_computation.80 | loop fusion | flops 655360 | bytes 2949120 | tf_op jit(solution)/shard_map/convert_element_type | solution.py:110
  93.4 3.9 %collective-permute-done.6 = f32[512,320]{0,1:T(8,128)S(1)} collective-permute-done((f32[512,320]{0,1:T(8,128)S(1)}, f32[512,320]{0,1:T(8,128)S(1)}, u32[]{:S(2)}, u32[]{:S(2)}) %collective-permute-start.6) | collective-permute-done | bytes 655392 | tf_op jit(solution)/shard_map/ppermute | solution.py:13
  97.2 18.4 %collective-permute-done.7 = f32[512,320]{0,1:T(8,128)S(1)} collective-permute-done((f32[512,320]{0,1:T(8,128)S(1)}, f32[512,320]{0,1:T(8,128)S(1)}, u32[]{:S(2)}, u32[]{:S(2)}) %collective-permute-start.7) | collective-permute-done | bytes 655392 | tf_op jit(solution)/shard_map/ppermute | solution.py:13
  115.7 14.0 %collective-permute-done.8 = f32[512,320]{0,1:T(8,128)S(1)} collective-permute-done((f32[512,320]{0,1:T(8,128)S(1)}, f32[512,320]{0,1:T(8,128)S(1)}, u32[]{:S(2)}, u32[]{:S(2)}) %collective-permute-start.8) | collective-permute-done | bytes 655392 | tf_op jit(solution)/shard_map/ppermute | solution.py:13
  129.7 2.1 %fusion.40 = bf16[512,320]{0,1:T(8,128)(2,1)} fusion(f32[512,320]{0,1:T(8,128)S(1)} %collective-permute-done.8, f32[512,320]{0,1:T(8,128)S(1)} %collective-permute-done.7, f32[512,320]{0,1:T(8,128)S(1)} %collective-permute-done.6, f32[2048,320]{0,1:T(8,128)} %convolution_dynamic-update-slice_fusion.5), kind=kLoop, calls=%fused_computation.84 | loop fusion | flops 655360 | bytes 2949120 | tf_op jit(solution)/shard_map/convert_element_type | solution.py:109
  131.8 16.5 %reduce-scatter.2.cloned.1.call-done = f32[256,320]{0,1:T(8,128)} async-done(((f32[256,1280]{0,1:T(8,128)}), f32[256,320]{0,1:T(8,128)}) %reduce-scatter.2.cloned.1.call-update) | async-done | bytes 327696 | tf_op jit(solution)/shard_map/reduce_scatter | solution.py:103
  148.3 1.7 %convert_element_type.112 = bf16[256,320]{0,1:T(8,128)(2,1)} convert(f32[256,320]{0,1:T(8,128)} %reduce-scatter.2.cloned.1.call-done) | non-fusion elementwise | flops 81920 | bytes 491520 | tf_op jit(solution)/shard_map/convert_element_type | solution.py:103
  (81 shorter events, 15.0 us)
Async XLA Ops:
  7.2 24.8 %copy-start = (bf16[320,1280]{1,0:T(8,128)(2,1)S(1)}, bf16[320,1280]{1,0:T(8,128)(2,1)}, u32[]{:S(2)}) copy-start(bf16[320,1280]{1,0:T(8,128)(2,1)} %param.9) | copy-start | bytes 2457604
  7.2 28.2 %copy-start.8 = (bf16[512,320]{0,1:T(8,128)(2,1)S(1)}, bf16[512,320]{0,1:T(8,128)(2,1)}, u32[]{:S(2)}) copy-start(bf16[512,320]{0,1:T(8,128)(2,1)} %param.7) | copy-start | bytes 983044
  7.2 25.2 %copy-start.9 = (bf16[512,320]{0,1:T(8,128)(2,1)S(1)}, bf16[512,320]{0,1:T(8,128)(2,1)}, u32[]{:S(2)}) copy-start(bf16[512,320]{0,1:T(8,128)(2,1)} %param.8) | copy-start | bytes 983044
  7.2 141.1 %reduce-scatter.2.cloned.1.call-start = ((), (), s32[]{:S(2)}) async-start(), calls=%async_computation.1 | async-start | bytes 1638400 | tf_op jit(solution)/shard_map/reduce_scatter | solution.py:103
  7.2 25.2 %collective-permute-start = (bf16[512,320]{0,1:T(8,128)(2,1)}, bf16[512,320]{0,1:T(8,128)(2,1)}, u32[]{:S(2)}, u32[]{:S(2)}) collective-permute-start(bf16[512,320]{0,1:T(8,128)(2,1)} %param.7), channel_id=1, source_target_pairs={{0,4},{4,8},{8,12},{12,16},{16,20},{20,24},{24,28},{28,32},{32,36}... | collective-permute-start | bytes 983048 | tf_op jit(solution)/shard_map/ppermute | solution.py:13
  10.6 24.8 %collective-permute-start.1 = (bf16[512,320]{0,1:T(8,128)(2,1)}, bf16[512,320]{0,1:T(8,128)(2,1)S(1)}, u32[]{:S(2)}, u32[]{:S(2)}) collective-permute-start(bf16[512,320]{0,1:T(8,128)(2,1)} %param.7), channel_id=1, source_target_pairs={{4,0},{8,4},{12,8},{16,12},{20,16},{24,20},{28,24},{32,28},{36,32}... | collective-permute-start | bytes 983048 | tf_op jit(solution)/shard_map/ppermute | solution.py:13
  12.7 22.8 %collective-permute-start.2 = (bf16[512,320]{0,1:T(8,128)(2,1)}, bf16[512,320]{0,1:T(8,128)(2,1)S(1)}, u32[]{:S(2)}, u32[]{:S(2)}) collective-permute-start(bf16[512,320]{0,1:T(8,128)(2,1)} %param.7), channel_id=1, source_target_pairs={{8,0},{12,4},{16,8},{20,12},{24,16},{28,20},{32,24},{36,28},{40,32... | collective-permute-start | bytes 983048 | tf_op jit(solution)/shard_map/ppermute | solution.py:13
  16.2 38.2 %collective-permute-start.3 = (bf16[512,320]{0,1:T(8,128)(2,1)}, bf16[512,320]{0,1:T(8,128)(2,1)S(1)}, u32[]{:S(2)}, u32[]{:S(2)}) collective-permute-start(bf16[512,320]{0,1:T(8,128)(2,1)} %param.8), channel_id=1, source_target_pairs={{0,4},{4,8},{8,12},{12,16},{16,20},{20,24},{24,28},{28,32},{32,36}... | collective-permute-start | bytes 983048 | tf_op jit(solution)/shard_map/ppermute | solution.py:13
  20.3 36.3 %collective-permute-start.4 = (bf16[512,320]{0,1:T(8,128)(2,1)}, bf16[512,320]{0,1:T(8,128)(2,1)S(1)}, u32[]{:S(2)}, u32[]{:S(2)}) collective-permute-start(bf16[512,320]{0,1:T(8,128)(2,1)} %param.8), channel_id=1, source_target_pairs={{4,0},{8,4},{12,8},{16,12},{20,16},{24,20},{28,24},{32,28},{36,32}... | collective-permute-start | bytes 983048 | tf_op jit(solution)/shard_map/ppermute | solution.py:13
  31.9 3.6 %copy-start.10 = (bf16[256,320]{0,1:T(8,128)(2,1)S(1)}, bf16[256,320]{0,1:T(8,128)(2,1)}, u32[]{:S(2)}) copy-start(bf16[256,320]{0,1:T(8,128)(2,1)} %param.6) | copy-start | bytes 491524
  32.4 24.2 %collective-permute-start.5 = (bf16[512,320]{0,1:T(8,128)(2,1)S(1)}, bf16[512,320]{0,1:T(8,128)(2,1)S(1)}, u32[]{:S(2)}, u32[]{:S(2)}) collective-permute-start(bf16[512,320]{0,1:T(8,128)(2,1)S(1)} %copy-done.9), channel_id=1, source_target_pairs={{8,0},{12,4},{16,8},{20,12},{24,16},{28,20},{32,24},{36,28},{40,32... | collective-permute-start | bytes 983048 | tf_op jit(solution)/shard_map/ppermute | solution.py:13
  35.5 2.6 %copy-start.6 = (bf16[2048,320]{0,1:T(8,128)(2,1)}, bf16[2048,320]{0,1:T(8,128)(2,1)S(1)}, u32[]{:S(2)}) copy-start(bf16[2048,320]{0,1:T(8,128)(2,1)S(1)} %constant_dynamic-update-slice_fusion.4) | copy-start | bytes 3932164
  43.0 13.6 %copy-start.5 = (f32[2048,320]{0,1:T(8,128)}, f32[2048,320]{0,1:T(8,128)S(1)}, u32[]{:S(2)}) copy-start(f32[2048,320]{0,1:T(8,128)S(1)} %convolution_dynamic-update-slice_fusion) | copy-start | bytes 7864324
  44.4 39.5 %collective-permute-start.10 = (f32[512,320]{0,1:T(8,128)}, f32[512,320]{0,1:T(8,128)}, u32[]{:S(2)}, u32[]{:S(2)}) collective-permute-start(f32[512,320]{0,1:T(8,128)} %get-tuple-element.13), channel_id=1, source_target_pairs={{0,4},{4,8},{8,12},{12,16},{16,20},{20,24},{24,28},{28,32},{32,36}... | collective-permute-start | bytes 1966088 | tf_op jit(solution)/shard_map/ppermute | solution.py:13
  50.1 40.6 %collective-permute-start.11 = (f32[512,320]{0,1:T(8,128)}, f32[512,320]{0,1:T(8,128)}, u32[]{:S(2)}, u32[]{:S(2)}) collective-permute-start(f32[512,320]{0,1:T(8,128)} %get-tuple-element.12), channel_id=1, source_target_pairs={{0,8},{4,12},{8,16},{12,20},{16,24},{20,28},{24,32},{28,36},{32,40... | collective-permute-start | bytes 1966088 | tf_op jit(solution)/shard_map/ppermute | solution.py:13
  54.4 36.3 %collective-permute-start.9 = (f32[512,320]{0,1:T(8,128)}, f32[512,320]{0,1:T(8,128)}, u32[]{:S(2)}, u32[]{:S(2)}) collective-permute-start(f32[512,320]{0,1:T(8,128)} %get-tuple-element.11), channel_id=1, source_target_pairs={{4,0},{8,4},{12,8},{16,12},{20,16},{24,20},{28,24},{32,28},{36,32}... | collective-permute-start | bytes 1966088 | tf_op jit(solution)/shard_map/ppermute | solution.py:13
  59.8 3.0 %copy-start.1 = (bf16[256,2048]{0,1:T(8,128)(2,1)}, bf16[256,2048]{0,1:T(8,128)(2,1)S(1)}, u32[]{:S(2)}) copy-start(bf16[256,2048]{0,1:T(8,128)(2,1)S(1)} %fusion.24) | copy-start | bytes 3145732
  65.8 1.7 %copy-start.11 = (bf16[256,320]{0,1:T(8,128)(2,1)S(1)}, bf16[256,320]{0,1:T(8,128)(2,1)}, u32[]{:S(2)}) copy-start(bf16[256,320]{0,1:T(8,128)(2,1)} %param.6) | copy-start | bytes 491524
  67.5 2.6 %copy-start.4 = (bf16[256,2048]{0,1:T(8,128)(2,1)S(1)}, bf16[256,2048]{0,1:T(8,128)(2,1)}, u32[]{:S(2)}) copy-start(bf16[256,2048]{0,1:T(8,128)(2,1)} %fusion.22) | copy-start | bytes 3145732
  73.8 9.2 %copy-start.2 = (bf16[256,2048]{0,1:T(8,128)(2,1)S(1)}, bf16[256,2048]{0,1:T(8,128)(2,1)}, u32[]{:S(2)}) copy-start(bf16[256,2048]{0,1:T(8,128)(2,1)} %copy-done.1) | copy-start | bytes 3145732
  73.8 9.2 %copy-start.7 = (bf16[2048,320]{0,1:T(8,128)(2,1)S(1)}, bf16[2048,320]{0,1:T(8,128)(2,1)}, u32[]{:S(2)}) copy-start(bf16[2048,320]{0,1:T(8,128)(2,1)} %copy-done.6) | copy-start | bytes 3932164
  73.8 9.5 %copy-start.3 = (bf16[256,2048]{0,1:T(8,128)(2,1)S(1)}, bf16[256,2048]{0,1:T(8,128)(2,1)}, u32[]{:S(2)}) copy-start(bf16[256,2048]{0,1:T(8,128)(2,1)} %fusion.23) | copy-start | bytes 3145732
  75.6 21.6 %collective-permute-start.6 = (f32[512,320]{0,1:T(8,128)S(1)}, f32[512,320]{0,1:T(8,128)S(1)}, u32[]{:S(2)}, u32[]{:S(2)}) collective-permute-start(f32[512,320]{0,1:T(8,128)S(1)} %get-tuple-element.14), channel_id=1, source_target_pairs={{4,0},{8,4},{12,8},{16,12},{20,16},{24,20},{28,24},{32,28},{36,32}... | collective-permute-start | bytes 1966088 | tf_op jit(solution)/shard_map/ppermute | solution.py:13
  78.6 37.0 %collective-permute-start.7 = (f32[512,320]{0,1:T(8,128)S(1)}, f32[512,320]{0,1:T(8,128)S(1)}, u32[]{:S(2)}, u32[]{:S(2)}) collective-permute-start(f32[512,320]{0,1:T(8,128)S(1)} %get-tuple-element.16), channel_id=1, source_target_pairs={{0,4},{4,8},{8,12},{12,16},{16,20},{20,24},{24,28},{28,32},{32,36}... | collective-permute-start | bytes 1966088 | tf_op jit(solution)/shard_map/ppermute | solution.py:13
  83.9 45.8 %collective-permute-start.8 = (f32[512,320]{0,1:T(8,128)S(1)}, f32[512,320]{0,1:T(8,128)S(1)}, u32[]{:S(2)}, u32[]{:S(2)}) collective-permute-start(f32[512,320]{0,1:T(8,128)S(1)} %get-tuple-element.15), channel_id=1, source_target_pairs={{0,8},{4,12},{8,16},{12,20},{16,24},{20,28},{24,32},{28,36},{32,40... | collective-permute-start | bytes 1966088 | tf_op jit(solution)/shard_map/ppermute | solution.py:13
  87.6 44.1 %copy-start.12 = (bf16[256,320]{0,1:T(8,128)(2,1)}, bf16[256,320]{0,1:T(8,128)(2,1)S(1)}, u32[]{:S(2)}) copy-start(bf16[256,320]{0,1:T(8,128)(2,1)S(1)} %fusion.30) | copy-start | bytes 491524
Sparse Core Ops, SparseCore 0:
  67.6 80.6 reduce-scatter.1
where the time goes:
time: 157 us
  waiting for transfers between devices  55.9 us (36%)
  starting transfers between devices  39.5 us (25%)
  matrix products  24.3 us (15%)
  between operations  14.5 us (9%)
  blocking collectives  8.77 us (6%)
  other arithmetic  8.27 us (5%)
  local copies, waits for them, and re-layouts  5.52 us (4%)
    ppermute x12, starting transfers between devices, passed_along(): return lax.ppermute(value, axis, pairs)  39.4 us
    ppermute x12, waiting for transfers between devices, passed_along(): return lax.ppermute(value, axis, pairs)  39.4 us
    reduce_scatter x1, waiting for transfers between devices, on_device(): lax.psum_scatter(partial_value, 'mp', scatter_dimension=1, tiled=True)  16.5 us
    dot_general x10, matrix products, dot_cols(): lax.dot_general(first_op, second_op, (((0,), (0,)), ((), ())), preferred_...  9.9 us
    dot_general x11, matrix products, dot_rows(): lax.dot_general(first_op, second_op, (((1,), (1,)), ((), ())), preferred_...  9.02 us
    all_gather x1, blocking collectives, on_device(): lax.all_gather(grad_out, 'mp', axis=1, tiled=True)  8.77 us
  transfers between devices with their start and end apart: 13, of which 5 were waited for; matrix products, arithmetic and copies ran while one was open for 23% of the time, Pallas kernels for 0%

commit v1 on v0

v1 whole, which is shorter than its diff:
```python
import jax
import jax.numpy as jnp
from jax import lax
from jax.experimental import pallas as pl
from jax.experimental.pallas import tpu as pltpu
from jax.sharding import PartitionSpec as P

DH = 64
BLK = 128
PAIR = 2 * DH
LOG2E = 1.4426950408889634
NT = (((1,), (1,)), ((), ()))
NN = (((1,), (0,)), ((), ()))
VMEM = pl.BlockSpec(memory_space=pltpu.VMEM)
SMEM = pl.BlockSpec(memory_space=pltpu.SMEM)
PARAMS = pltpu.CompilerParams(vmem_limit_bytes=40 * 1024 * 1024)


def ring(value, by):
    count = lax.axis_size("seq")
    return lax.ppermute(value, "seq", [(i, (i + by) % count) for i in range(count)])


def dot(first_op, second_op, dims):
    return lax.dot_general(first_op, second_op, dims, preferred_element_type=jnp.float32)


def halves(pair):
    lane = lax.broadcasted_iota(jnp.int32, pair.shape, 1)
    zero = jnp.zeros_like(pair)
    return jnp.where(lane < DH, pair, zero), jnp.where(lane < DH, zero, pair)


def pack_frames(keys_ref, values_ref, out_ref):
    for head in range(out_ref.shape[0]):
        cols = slice(head * DH, (head + 1) * DH)
        out_ref[head] = jnp.concatenate([keys_ref[:, cols], values_ref[:, cols]], axis=1)


def pack_tokens(grad_ref, weight_ref, queries_ref, out_ref):
    grad = dot(grad_ref[...], weight_ref[...], NT).astype(jnp.bfloat16)
    for head in range(out_ref.shape[0]):
        cols = slice(head * DH, (head + 1) * DH)
        out_ref[head] = jnp.concatenate([queries_ref[:, cols], grad[:, cols]], axis=1)


def window_bias(rel_ref, frames, tokens):
    block = lax.broadcasted_iota(jnp.int32, (1, frames), 1) // BLK
    rows = [
        jnp.where((block >= rel_ref[g, 0]) & (block < rel_ref[g, 1]), 0.0, -jnp.inf).astype(
            jnp.float32
        )
        for g in range(tokens // BLK)
    ]
    return rows


def forward(
    rel_ref, align_ref, pair_ref, f0, f1, f2, f3, attended_ref, cols_ref, rows_ref, work
):
    heads, tokens, _ = pair_ref.shape
    slots = (f0, f1, f2, f3)
    span = f0.shape[1]
    scale = LOG2E * DH ** (-0.5)
    bias = window_bias(rel_ref, 4 * span, tokens)
    lane = lax.broadcasted_iota(jnp.int32, (tokens, 128), 1)
    row = lax.broadcasted_iota(jnp.int32, (tokens, 128), 0)
    lower = jnp.where(row < BLK, align_ref[0, 0], align_ref[1, 0]).astype(jnp.float32)
    upper = jnp.where(row < BLK, align_ref[0, 1], align_ref[1, 1]).astype(jnp.float32)
    stats = jnp.where(lane == 2 * heads, lower, jnp.where(lane == 2 * heads + 1, upper, 0.0))
    for head in range(heads):
        pair = pair_ref[head]
        query, _ = halves(pair)
        for g in range(tokens // BLK):
            rows = slice(g * BLK, (g + 1) * BLK)
            top = None
            for s, slot in enumerate(slots):
                raw = dot(query[rows], slot[head], NT) * scale + bias[g][:, s * span : (s + 1) * span]
                work[:, s * span : (s + 1) * span] = raw
                for c in range(0, span, 128):
                    part = raw[:, c : c + 128]
                    top = part if top is None else jnp.maximum(top, part)
            top = jnp.max(top, axis=1, keepdims=True)
            total = None
            for s in range(4):
                prob = jnp.exp2(work[:, s * span : (s + 1) * span] - top)
                work[:, s * span : (s + 1) * span] = prob
                for c in range(0, span, 128):
                    part = prob[:, c : c + 128]
                    total = part if total is None else total + part
            total = jnp.sum(total, axis=1, keepdims=True)
            inverse = 1.0 / total
            logsum = top + jnp.log2(total)
            out = None
            for s, slot in enumerate(slots):
                low = (work[:, s * span : (s + 1) * span] * inverse).astype(jnp.bfloat16)
                part = dot(low, slot[head], NN)
                out = part if out is None else out + part
            low_out = out.astype(jnp.bfloat16)
            attended_ref[rows, head * DH : (head + 1) * DH] = low_out[:, DH:]
            product = jnp.where(
                lane[rows] < DH, 0.0, low_out.astype(jnp.float32) * pair[rows].astype(jnp.float32)
            )
            delta = jnp.sum(product, axis=1, keepdims=True)
            part = stats[rows] if head == 0 else cols_ref[rows, :]
            part = jnp.where(lane[rows] == head, logsum, part)
            cols_ref[rows, :] = jnp.where(lane[rows] == heads + head, delta, part)
    rows_ref[...] = cols_ref[...].T[: rows_ref.shape[0]]


def query_side(rel_ref, pair_ref, cols_ref, f0, f1, f2, f3, grad_ref):
    heads, tokens, _ = pair_ref.shape
    slots = (f0, f1, f2, f3)
    span = f0.shape[1]
    factor = DH ** (-0.5)
    bias = window_bias(rel_ref, 4 * span, tokens)
    for head in range(heads):
        query, grad = halves(pair_ref[head])
        for g in range(tokens // BLK):
            rows = slice(g * BLK, (g + 1) * BLK)
            logsum = cols_ref[rows, head : head + 1]
            delta = cols_ref[rows, heads + head : heads + head + 1]
            out = None
            for s, slot in enumerate(slots):
                frame = slot[head]
                raw = dot(query[rows], frame, NT) * (LOG2E * factor)
                prob = jnp.exp2(raw + bias[g][:, s * span : (s + 1) * span] - logsum)
                dprob = dot(grad[rows], frame, NT)
                low = (prob * (dprob - delta)).astype(jnp.bfloat16)
                part = dot(low, frame, NN)
                out = part if out is None else out + part
            grad_ref[rows, head * DH : (head + 1) * DH] = (out[:, :DH] * factor).astype(jnp.bfloat16)


def frame_side(
    place_ref, own_ref, p0, p1, p2, p3, s0, s1, s2, s3, key_grad_ref, value_grad_ref
):
    heads, span, _ = own_ref.shape
    tokens = p0.shape[1]
    factor = DH ** (-0.5)
    first = place_ref[0]
    sources = ((p0, s0), (p1, s1), (p2, s2), (p3, s3))
    bias = []
    for _, stat in sources:
        lower, upper = (stat[2 * heads : 2 * heads + 1, :], stat[2 * heads + 1 : 2 * heads + 2, :])
        per = []
        for b in range(span // BLK):
            block = (first + b).astype(jnp.float32)
            per.append(jnp.where((lower <= block) & (block < upper), 0.0, -jnp.inf))
        bias.append(per)
    for head in range(heads):
        frame = own_ref[head]
        out = None
        for j, (pair_ref, stat) in enumerate(sources):
            both = jnp.concatenate(halves(pair_ref[head]), axis=0)
            logsum = stat[head : head + 1, :]
            delta = stat[heads + head : heads + head + 1, :]
            raw = dot(frame, both, NT)
            lows = []
            for b in range(span // BLK):
                rows = slice(b * BLK, (b + 1) * BLK)
                prob = jnp.exp2(raw[rows, :tokens] * (LOG2E * factor) + (bias[j][b] - logsum))
                dscore = prob * (raw[rows, tokens:] - delta)
                lows.append(
                    jnp.concatenate(
                        [dscore.astype(jnp.bfloat16), prob.astype(jnp.bfloat16)], axis=1
                    )
                )
            part = dot(jnp.concatenate(lows, axis=0), both, NN)
            out = part if out is None else out + part
        cols = slice(head * DH, (head + 1) * DH)
        key_grad_ref[:, cols] = (out[:, :DH] * factor).astype(jnp.bfloat16)
        value_grad_ref[:, cols] = out[:, DH:].astype(jnp.bfloat16)


def after(value, *others):
    return lax.optimization_barrier((value,) + others)[0]


def on_device(queries, keys, values, out_weight, grad_out, alignment):
    frames, feats = keys.shape
    tokens = queries.shape[0]
    heads = feats // DH
    frame_blocks = frames // BLK
    position = lax.axis_index("seq").astype(jnp.int32)
    shape = jax.ShapeDtypeStruct
    bf16, f32 = jnp.bfloat16, jnp.float32

    with jax.named_scope("pack_frames"):
        frame_pack = pl.pallas_call(
            pack_frames,
            out_shape=shape((heads, frames, PAIR), bf16),
            in_specs=[VMEM] * 2,
            out_specs=VMEM,
            compiler_params=PARAMS,
        )(keys, values)
    window = [ring(frame_pack, 1), frame_pack, ring(frame_pack, -1), ring(frame_pack, -2)]

    grad_all = lax.all_gather(grad_out, "mp", axis=1, tiled=True)
    with jax.named_scope("pack_tokens"):
        token_pack = pl.pallas_call(
            pack_tokens,
            out_shape=shape((heads, tokens, PAIR), bf16),
            in_specs=[VMEM] * 3,
            out_specs=VMEM,
            compiler_params=PARAMS,
        )(grad_all, out_weight, queries)
    weight_cols = lax.all_to_all(out_weight, "mp", 1, 0, tiled=True)

    sent_pack = after(token_pack, *window)
    token_packs = [ring(sent_pack, 1), ring(sent_pack, -1), ring(sent_pack, 2)]

    relative = alignment - (position - 1) * frame_blocks
    with jax.named_scope("forward"):
        attended, stat_cols, stat_rows = pl.pallas_call(
            forward,
            out_shape=(
                shape((tokens, feats), bf16),
                shape((tokens, 128), f32),
                shape((16, tokens), f32),
            ),
            in_specs=[SMEM] * 2 + [VMEM] * 5,
            out_specs=(VMEM,) * 3,
            scratch_shapes=[pltpu.VMEM((BLK, 4 * frames), f32)],
            compiler_params=PARAMS,
        )(relative, alignment, token_pack, *window)
    stats = [ring(stat_rows, 1), ring(stat_rows, -1), ring(stat_rows, 2)]

    attended_all = lax.all_gather(attended, "mp", axis=1, tiled=True)
    layer_output = dot(attended_all, weight_cols, NN).astype(bf16)

    with jax.named_scope("query_side"):
        query_grad = pl.pallas_call(
            query_side,
            out_shape=shape((tokens, feats), bf16),
            in_specs=[SMEM] + [VMEM] * 6,
            out_specs=VMEM,
            compiler_params=PARAMS,
        )(relative, token_pack, stat_cols, *window)

    with jax.named_scope("frame_side"):
        key_grad, value_grad = pl.pallas_call(
            frame_side,
            out_shape=(shape((frames, feats), bf16),) * 2,
            in_specs=[SMEM] + [VMEM] * 9,
            out_specs=(VMEM,) * 2,
            compiler_params=PARAMS,
        )(
            (position * frame_blocks).reshape(1),
            frame_pack,
            token_pack,
            *token_packs,
            stat_rows,
            *stats,
        )
    return layer_output, query_grad, key_grad, value_grad


def solution(mesh):
    return jax.shard_map(
        on_device,
        mesh=mesh,
        in_specs=(
            P("seq", "mp"),
            P("seq", "mp"),
            P("seq", "mp"),
            P("mp", None),
            P("seq", "mp"),
            P("seq", None),
        ),
        out_specs=(P("seq", "mp"), P("seq", "mp"), P("seq", "mp"), P("seq", "mp")),
        check_vma=False,
    )
```

time: 157 us -> 112 us (0.71)
  the two profiles are of different devices: /device:TPU:27 before, /device:TPU:185 now
where the time goes in v1:
time: 112 us; the launch traced here: 111 us
  starting transfers between devices  40.2 us (36%)
  blocking collectives  26.5 us (24%)
  Pallas kernels  24.9 us (22%)
  local copies, waits for them, and re-layouts  17.8 us (16%)
    ppermute x9, starting transfers between devices, ring(): lax.ppermute(value, 'seq', [(i, (i + by) % count) for i in range(count)])  34.4 us
    all_gather x1, blocking collectives, on_device(): grad_all = lax.all_gather(grad_out, 'mp', axis=1, tiled=True)  17.5 us
    unnamed x25, local copies, waits for them, and re-layouts  9.14 us
    all_gather x1, blocking collectives, on_device(): attended_all = lax.all_gather(attended, 'mp', axis=1, tiled=True)  9 us
    pallas_call x1, Pallas kernels, on_device(): pl.pallas_call(query_side, out_shape=shape((tokens, feats), bf16), in_spe...  8.52 us
    pallas_call x1, Pallas kernels, on_device(): pl.pallas_call(forward, out_shape=(shape((tokens, feats), bf16), shape((t...  8.31 us
    pallas_call x1, Pallas kernels, on_device(): pl.pallas_call(frame_side, out_shape=(shape((frames, feats), bf16),) * 2,...  7.2 us
    all_to_all x1, starting transfers between devices, on_device(): weight_cols = lax.all_to_all(out_weight, 'mp', 1, 0, tiled=True)  5.83 us
  transfers between devices with their start and end apart: 10, of which 0 were waited for; matrix products, arithmetic and copies ran while one was open for 8% of the time, Pallas kernels for 16%

profile of v1, /device:TPU:185, one launch (start us, length us, event | category | flops | bytes accessed | tf_op | source)
XLA Modules:
  0.0 111.2 jit_solution(548677125440550342)
XLA Ops:
  0.6 1.2 %copy.27.keys_ref = bf16[512,320]{1,0:T(8,128)(2,1)S(1)} copy(bf16[512,320]{0,1:T(8,128)(2,1)} %param.7) | data formatting | bytes 655360 | tf_op args[1]
  1.9 0.2 copy.28.values_ref
  2.1 0.2 pack_frames.1.f1.own_ref
  2.4 1.0 collective-permute-start.2
  3.4 3.6 %collective-permute-start = (bf16[5,512,128]{2,1,0:T(8,128)(2,1)S(1)}, bf16[5,512,128]{2,1,0:T(8,128)(2,1)}, u32[]{:S(2)}, u32[]{:S(2)}) collective-permute-start(bf16[5,512,128]{2,1,0:T(8,128)(2,1)S(1)} %pack_frames.1.f1.own_ref), channel_id=1, source_target_pairs={{0,4},{4,8},{8,12},{12,16},{16,20},{20,24},{24,28},{28,32},{32,36}... | collective-permute-start | bytes 1966088 | tf_op jit(solution)/shard_map/ppermute | solution.py:21
  7.0 1.3 %copy.30 = bf16[320,1280]{0,1:T(8,128)(2,1)} copy(bf16[320,1280]{1,0:T(8,128)(2,1)S(1)} %copy-done) | data formatting | bytes 1638400 | tf_op args[3]
  8.3 5.8 %all-to-all-start = ((bf16[320,4,320]{0,2,1:T(8,128)(2,1)}), bf16[320,4,320]{0,2,1:T(8,128)(2,1)}, u32[]{:S(2)}, u32[]{:S(2)}) async-start(bf16[320,4,320]{0,2,1:T(8,128)(2,1)} %bitcast.7), calls=%async_computation | async-start | bytes 1966080 | tf_op jit(solution)/shard_map/all_to_all | solution.py:208
  14.1 0.2 copy.26.queries_ref
  14.3 0.7 copy-done.8
  15.0 17.5 %all_gather.6 = bf16[256,1280]{0,1:T(8,128)(2,1)} all-gather(bf16[256,320]{0,1:T(8,128)(2,1)S(1)} %copy-done.8), channel_id=1, replica_groups=mesh['seq'=64,'mp'=4] {'mp'}, dimensions={1}, use_global_device_ids=true | all-gather | bytes 819200 | tf_op jit(solution)/shard_map/all_gather | solution.py:199
  32.5 2.2 %copy.25.grad_ref = bf16[256,1280]{1,0:T(8,128)(2,1)} copy(bf16[256,1280]{0,1:T(8,128)(2,1)} %all_gather.6) | data formatting | bytes 1310720 | tf_op jit(solution)/shard_map/all_gather | solution.py:199
  34.7 1.1 copy-done.1
  35.8 0.6 pack_tokens.1.pair_ref.p0
  36.4 0.1 copy-done.4
  36.5 2.9 %copy.31 = bf16[4,320,320]{1,0,2:T(4,128)(2,1)} copy(bf16[4,320,320]{1,2,0:T(8,128)(2,1)} %bitcast.1) | data formatting | bytes 1638400 | tf_op jit(solution)/shard_map/all_to_all | solution.py:208
  39.4 2.7 %all_to_all.17 = bf16[1280,320]{0,1:T(8,128)(2,1)} reshape(bf16[4,320,320]{1,0,2:T(4,128)(2,1)} %copy.31) | data formatting | bytes 1638400 | tf_op jit(solution)/shard_map/all_to_all | solution.py:208
  42.2 0.9 collective-permute-start.5
  43.1 0.5 collective-permute-start.4
  43.5 3.1 %collective-permute-start.3 = (bf16[5,256,128]{2,1,0:T(8,128)(2,1)S(1)}, bf16[5,256,128]{2,1,0:T(8,128)(2,1)}, u32[]{:S(2)}, u32[]{:S(2)}) collective-permute-start(bf16[5,256,128]{2,1,0:T(8,128)(2,1)S(1)} %pack_tokens.1.pair_ref.p0), channel_id=1, source_target_pairs={{0,4},{4,8},{8,12},{12,16},{16,20},{20,24},{24,28},{28,32},{32,36}... | collective-permute-start | bytes 983048 | tf_op jit(solution)/shard_map/ppermute | solution.py:21
  46.6 8.3 %forward.1 = (bf16[256,320]{1,0:T(8,128)(2,1)S(1)}, f32[256,128]{1,0:T(8,128)S(1)}, f32[16,256]{1,0:T(8,128)S(1)}) custom-call(s32[2,2]{1,0:T(2,128)S(1)} %broadcast_subtract_fusion.rel_ref, s32[2,2]{1,0:T(2,128)S(1)} %copy-done.4, bf16[5,256,128]{2,1,0:T(8,128)(2,1)S(1)} %pack_tokens.1.pair_ref.p0, bf16[5,512,128]{2,1,0:T(8,128)(2,1)} %collective-permute-done.f0, ...), custom_call_target="tpu_custom_call" | custom-call | tf_op jit(solution)/shard_map/forward/pallas_call | solution.py:215
  54.9 21.5 %collective-permute-start.8 = (f32[16,256]{1,0:T(8,128)S(1)}, f32[16,256]{1,0:T(8,128)S(1)}, u32[]{:S(2)}, u32[]{:S(2)}) collective-permute-start(f32[16,256]{1,0:T(8,128)S(1)} %get-tuple-element.13.s0), channel_id=1, source_target_pairs={{0,8},{4,12},{8,16},{12,20},{16,24},{20,28},{24,32},{28,36},{32,40... | collective-permute-start | bytes 49160 | tf_op jit(solution)/shard_map/ppermute | solution.py:21
  76.4 0.8 copy.29
  77.2 9.0 %all_gather.7 = bf16[256,1280]{0,1:T(8,128)(2,1)S(1)} all-gather(bf16[256,320]{0,1:T(8,128)(2,1)} %copy.29), channel_id=1, replica_groups=mesh['seq'=64,'mp'=4] {'mp'}, dimensions={1}, use_global_device_ids=true | all-gather | bytes 819200 | tf_op jit(solution)/shard_map/all_gather | solution.py:229
  86.2 3.9 %collective-permute-start.6 = (f32[16,256]{1,0:T(8,128)S(1)}, f32[16,256]{1,0:T(8,128)S(1)}, u32[]{:S(2)}, u32[]{:S(2)}) collective-permute-start(f32[16,256]{1,0:T(8,128)S(1)} %get-tuple-element.13.s0), channel_id=1, source_target_pairs={{0,4},{4,8},{8,12},{12,16},{16,20},{20,24},{24,28},{28,32},{32,36}... | collective-permute-start | bytes 49160 | tf_op jit(solution)/shard_map/ppermute | solution.py:21
  90.1 1.1 convolution_convert_fusion
  91.1 8.5 %query_side.1 = bf16[256,320]{1,0:T(8,128)(2,1)S(1)} custom-call(s32[2,2]{1,0:T(2,128)S(1)} %broadcast_subtract_fusion.rel_ref, bf16[5,256,128]{2,1,0:T(8,128)(2,1)S(1)} %pack_tokens.1.pair_ref.p0, f32[256,128]{1,0:T(8,128)S(1)} %get-tuple-element.11.cols_ref, bf16[5,512,128]{2,1,0:T(8,128)(2,1)} %collective-permute-done.f0, ...), custom_call_target="tpu_custom_call" | custom-call | tf_op jit(solution)/shard_map/query_side/pallas_call | solution.py:233
  99.7 0.8 copy.32
  100.5 0.7 copy-done.2
  101.2 1.0 copy-done.3
  102.2 7.2 %frame_side.1 = (bf16[512,320]{1,0:T(8,128)(2,1)S(1)}, bf16[512,320]{1,0:T(8,128)(2,1)S(1)}) custom-call(s32[1]{0:T(128)} %bitcast.2.place_ref, bf16[5,512,128]{2,1,0:T(8,128)(2,1)S(1)} %pack_frames.1.f1.own_ref, bf16[5,256,128]{2,1,0:T(8,128)(2,1)S(1)} %pack_tokens.1.pair_ref.p0, bf16[5,256,128]{2,1,0:T(8,128)(2,1)} %collective-permute-done.3.p1, ...), custom_call_target="tpu_custom_call" | custom-call | tf_op jit(solution)/shard_map/frame_side/pallas_call | solution.py:242
  109.4 0.9 copy.33
  110.3 0.9 copy.34
  (26 shorter events, 0.1 us)
Async XLA Ops:
  0.6 1.2 %copy-start.6 = (bf16[512,320]{0,1:T(8,128)(2,1)S(1)}, bf16[512,320]{0,1:T(8,128)(2,1)}, u32[]{:S(2)}) copy-start(bf16[512,320]{0,1:T(8,128)(2,1)} %param.8) | copy-start | bytes 983044
  2.1 4.9 %copy-start = (bf16[320,1280]{1,0:T(8,128)(2,1)S(1)}, bf16[320,1280]{1,0:T(8,128)(2,1)}, u32[]{:S(2)}) copy-start(bf16[320,1280]{1,0:T(8,128)(2,1)} %weight_ref.1) | copy-start | bytes 2457604
  2.4 39.8 %collective-permute-start.2 = (bf16[5,512,128]{2,1,0:T(8,128)(2,1)S(1)}, bf16[5,512,128]{2,1,0:T(8,128)(2,1)S(1)}, u32[]{:S(2)}, u32[]{:S(2)}) collective-permute-start(bf16[5,512,128]{2,1,0:T(8,128)(2,1)S(1)} %pack_frames.1.f1.own_ref), channel_id=1, source_target_pairs={{0,248},{4,252},{8,0},{12,4},{16,8},{20,12},{24,16},{28,20},{32,24... | collective-permute-start | bytes 1966088 | tf_op jit(solution)/shard_map/ppermute | solution.py:21
  3.4 38.8 %collective-permute-start.1 = (bf16[5,512,128]{2,1,0:T(8,128)(2,1)S(1)}, bf16[5,512,128]{2,1,0:T(8,128)(2,1)S(1)}, u32[]{:S(2)}, u32[]{:S(2)}) collective-permute-start(bf16[5,512,128]{2,1,0:T(8,128)(2,1)S(1)} %pack_frames.1.f1.own_ref), channel_id=1, source_target_pairs={{0,252},{4,0},{8,4},{12,8},{16,12},{20,16},{24,20},{28,24},{32,28}... | collective-permute-start | bytes 1966088 | tf_op jit(solution)/shard_map/ppermute | solution.py:21
  3.4 38.8 %collective-permute-start = (bf16[5,512,128]{2,1,0:T(8,128)(2,1)S(1)}, bf16[5,512,128]{2,1,0:T(8,128)(2,1)}, u32[]{:S(2)}, u32[]{:S(2)}) collective-permute-start(bf16[5,512,128]{2,1,0:T(8,128)(2,1)S(1)} %pack_frames.1.f1.own_ref), channel_id=1, source_target_pairs={{0,4},{4,8},{8,12},{12,16},{16,20},{20,24},{24,28},{28,32},{32,36}... | collective-permute-start | bytes 1966088 | tf_op jit(solution)/shard_map/ppermute | solution.py:21
  8.3 5.8 %copy-start.7 = (bf16[256,320]{0,1:T(8,128)(2,1)S(1)}, bf16[256,320]{0,1:T(8,128)(2,1)}, u32[]{:S(2)}) copy-start(bf16[256,320]{0,1:T(8,128)(2,1)} %param.6) | copy-start | bytes 491524
  8.3 28.2 %all-to-all-start = ((bf16[320,4,320]{0,2,1:T(8,128)(2,1)}), bf16[320,4,320]{0,2,1:T(8,128)(2,1)}, u32[]{:S(2)}, u32[]{:S(2)}) async-start(bf16[320,4,320]{0,2,1:T(8,128)(2,1)} %bitcast.7), calls=%async_computation | async-start | bytes 1966080 | tf_op jit(solution)/shard_map/all_to_all | solution.py:208
  14.1 0.9 copy-start.8
  34.7 1.1 copy-start.1
  35.8 0.7 copy-start.4
  42.2 58.3 %collective-permute-start.5 = (bf16[5,256,128]{2,1,0:T(8,128)(2,1)S(1)}, bf16[5,256,128]{2,1,0:T(8,128)(2,1)S(1)}, u32[]{:S(2)}, u32[]{:S(2)}) collective-permute-start(bf16[5,256,128]{2,1,0:T(8,128)(2,1)S(1)} %pack_tokens.1.pair_ref.p0), channel_id=1, source_target_pairs={{0,8},{4,12},{8,16},{12,20},{16,24},{20,28},{24,32},{28,36},{32,40... | collective-permute-start | bytes 983048 | tf_op jit(solution)/shard_map/ppermute | solution.py:21
  43.1 57.4 %collective-permute-start.4 = (bf16[5,256,128]{2,1,0:T(8,128)(2,1)S(1)}, bf16[5,256,128]{2,1,0:T(8,128)(2,1)S(1)}, u32[]{:S(2)}, u32[]{:S(2)}) collective-permute-start(bf16[5,256,128]{2,1,0:T(8,128)(2,1)S(1)} %pack_tokens.1.pair_ref.p0), channel_id=1, source_target_pairs={{0,252},{4,0},{8,4},{12,8},{16,12},{20,16},{24,20},{28,24},{32,28}... | collective-permute-start | bytes 983048 | tf_op jit(solution)/shard_map/ppermute | solution.py:21
  43.5 57.7 %collective-permute-start.3 = (bf16[5,256,128]{2,1,0:T(8,128)(2,1)S(1)}, bf16[5,256,128]{2,1,0:T(8,128)(2,1)}, u32[]{:S(2)}, u32[]{:S(2)}) collective-permute-start(bf16[5,256,128]{2,1,0:T(8,128)(2,1)S(1)} %pack_tokens.1.pair_ref.p0), channel_id=1, source_target_pairs={{0,4},{4,8},{8,12},{12,16},{16,20},{20,24},{24,28},{28,32},{32,36}... | collective-permute-start | bytes 983048 | tf_op jit(solution)/shard_map/ppermute | solution.py:21
  54.9 31.3 %collective-permute-start.8 = (f32[16,256]{1,0:T(8,128)S(1)}, f32[16,256]{1,0:T(8,128)S(1)}, u32[]{:S(2)}, u32[]{:S(2)}) collective-permute-start(f32[16,256]{1,0:T(8,128)S(1)} %get-tuple-element.13.s0), channel_id=1, source_target_pairs={{0,8},{4,12},{8,16},{12,20},{16,24},{20,28},{24,32},{28,36},{32,40... | collective-permute-start | bytes 49160 | tf_op jit(solution)/shard_map/ppermute | solution.py:21
  76.4 24.0 %collective-permute-start.7 = (f32[16,256]{1,0:T(8,128)S(1)}, f32[16,256]{1,0:T(8,128)S(1)}, u32[]{:S(2)}, u32[]{:S(2)}) collective-permute-start(f32[16,256]{1,0:T(8,128)S(1)} %get-tuple-element.13.s0), channel_id=1, source_target_pairs={{0,252},{4,0},{8,4},{12,8},{16,12},{20,16},{24,20},{28,24},{32,28}... | collective-permute-start | bytes 49160 | tf_op jit(solution)/shard_map/ppermute | solution.py:21
  77.2 12.9 %copy-start.5 = (bf16[1280,320]{0,1:T(8,128)(2,1)S(1)}, bf16[1280,320]{0,1:T(8,128)(2,1)}, u32[]{:S(2)}) copy-start(bf16[1280,320]{0,1:T(8,128)(2,1)} %all_to_all.17) | copy-start | bytes 2457604
  86.2 14.2 %collective-permute-start.6 = (f32[16,256]{1,0:T(8,128)S(1)}, f32[16,256]{1,0:T(8,128)S(1)}, u32[]{:S(2)}, u32[]{:S(2)}) collective-permute-start(f32[16,256]{1,0:T(8,128)S(1)} %get-tuple-element.13.s0), channel_id=1, source_target_pairs={{0,4},{4,8},{8,12},{12,16},{16,20},{20,24},{24,28},{28,32},{32,36}... | collective-permute-start | bytes 49160 | tf_op jit(solution)/shard_map/ppermute | solution.py:21
  100.5 0.7 copy-start.2
  101.2 1.0 copy-start.3

commit v2 on v0

v2 whole, which is shorter than its diff:
```python
import jax
import jax.numpy as jnp
from jax import lax
from jax.experimental import pallas as pl
from jax.experimental.pallas import tpu as pltpu
from jax.sharding import PartitionSpec as P

DH = 64
BLK = 128
PAIR = 2 * DH
FACTOR = DH ** (-0.5)
LOG2E = 1.4426950408889634
FAR = -1e30
BIAS_ROWS = 16
TERMS = 3
STAT_ROWS = 16
NT = (((1,), (1,)), ((), ()))
NN = (((1,), (0,)), ((), ()))
VMEM = pl.BlockSpec(memory_space=pltpu.VMEM)
SMEM = pl.BlockSpec(memory_space=pltpu.SMEM)
HBM = pl.BlockSpec(memory_space=pltpu.HBM)
PARAMS = pltpu.CompilerParams(vmem_limit_bytes=20 * 1024 * 1024)


def ring(value, by):
    count = lax.axis_size("seq")
    return lax.ppermute(value, "seq", [(i, (i + by) % count) for i in range(count)])


def dot(first_op, second_op, dims):
    return lax.dot_general(first_op, second_op, dims, preferred_element_type=jnp.float32)


def iota(shape, dim):
    return lax.broadcasted_iota(jnp.int32, shape, dim)


def pack_frames(keys_ref, values_ref, out_ref, done):
    copies = []
    for head in range(out_ref.shape[0]):
        rows = pl.ds(head * DH, DH)
        for side, source in enumerate((keys_ref, values_ref)):
            target = out_ref.at[head, pl.ds(side * DH, DH)]
            copies.append(pltpu.make_async_copy(source.at[rows], target, done.at[side, head]))
    for copy in copies:
        copy.start()
    for copy in copies:
        copy.wait()


def pack_tokens(me_ref, own_ref, far_ref, other_ref, weight_ref, queries_ref, out_ref, whole):
    feats = own_ref.shape[0]
    parts = (own_ref[...], far_ref[...], other_ref[:feats], other_ref[feats:])
    for part, flip in zip(parts, (0, 2, 1, 3)):
        first = pl.multiple_of((me_ref[0] ^ flip) * feats, feats)
        whole[pl.ds(first, feats), :] = part
    grad = dot(weight_ref[...], whole[...], NN).astype(jnp.bfloat16)
    for head in range(out_ref.shape[0]):
        rows = slice(head * DH, (head + 1) * DH)
        out_ref[head, :DH] = queries_ref[rows]
        out_ref[head, DH:] = grad[rows]


def three_terms(row):
    high = row.astype(jnp.bfloat16).astype(jnp.float32)
    middle = (row - high).astype(jnp.bfloat16).astype(jnp.float32)
    return [high, middle, row - high - middle]


def padded(parts):
    have = sum(p.shape[0] for p in parts)
    zeros = jnp.zeros((DH - have, parts[0].shape[1]), jnp.float32)
    return jnp.concatenate(parts + [zeros], axis=0).astype(jnp.bfloat16)


def turned(parts):
    return jnp.concatenate(parts, axis=0).T


def block_bias(first_block, lower, upper):
    block = (first_block + iota((BIAS_ROWS, lower.shape[1]), 0)).astype(jnp.float32)
    return jnp.where((lower <= block) & (block < upper), 0.0, FAR)


def score_rows(frames, first_row):
    row = iota((DH, frames), 0)
    block = first_row + iota((DH, frames), 1) // BLK
    ones = jnp.where(row == block, 1.0, 0.0)
    minus = (row >= BIAS_ROWS) & (row < BIAS_ROWS + TERMS)
    return jnp.where(minus, -1.0, ones).astype(jnp.bfloat16)


def dprob_rows(frames):
    return jnp.where(iota((DH, frames), 0) < TERMS, -1.0, 0.0).astype(jnp.bfloat16)


def score_side(pair, bias, logsum):
    return turned([pair[:DH], padded([bias] + three_terms(logsum))])


def dprob_side(pair, delta):
    return turned([padded(three_terms(delta)), pair[DH:]])


def forward(place_ref, align_ref, pair_ref, f0, f1, f2, f3, attended_ref, stats_ref, work, sums):
    heads, _, tokens = pair_ref.shape
    slots = (f0, f1, f2, f3)
    span = f0.shape[2]
    lane = iota((1, tokens), 1)
    lower = jnp.where(lane < BLK, align_ref[0, 0], align_ref[1, 0]).astype(jnp.float32)
    upper = jnp.where(lane < BLK, align_ref[0, 1], align_ref[1, 1]).astype(jnp.float32)
    bias = block_bias(place_ref[0] - span // BLK, lower, upper)
    beside = [score_rows(span, s * (span // BLK)) for s in range(4)]
    units = [(head, g) for head in range(heads) for g in range(tokens // BLK)]
    sides = {}

    def scores(unit):
        head, g = units[unit]
        if g == 0:
            sides[head] = turned([pair_ref[head, :DH], padded([bias])])
        left = sides[head][g * BLK : (g + 1) * BLK]
        top = None
        for s, slot in enumerate(slots):
            raw = dot(left, jnp.concatenate([slot[head, :DH], beside[s]], axis=0), NN)
            work[unit % 3, :, s * span : (s + 1) * span] = raw
            for c in range(0, span, 128):
                part = raw[:, c : c + 128]
                top = part if top is None else jnp.maximum(top, part)
        return jnp.max(top, axis=1, keepdims=True)

    ahead = scores(0)
    for unit, (head, g) in enumerate(units):
        top = ahead
        if unit + 1 < len(units):
            ahead = scores(unit + 1)
        total = None
        for s in range(4):
            raw = work[unit % 3, :, s * span : (s + 1) * span]
            prob = jnp.exp2((raw - top) * (LOG2E * FACTOR))
            work[unit % 3, :, s * span : (s + 1) * span] = prob
            for c in range(0, span, 128):
                part = prob[:, c : c + 128]
                total = part if total is None else total + part
        total = jnp.sum(total, axis=1, keepdims=True)
        inverse = 1.0 / total
        cols = slice(g * BLK, (g + 1) * BLK)
        sums[cols, head : head + 1] = top + jnp.log(total) * (1.0 / FACTOR)
        out = None
        for s, slot in enumerate(slots):
            low = (work[unit % 3, :, s * span : (s + 1) * span] * inverse).astype(jnp.bfloat16)
            part = dot(low, slot[head, DH:], NT)
            out = part if out is None else out + part
        low_out = out.T.astype(jnp.bfloat16)
        attended_ref[head * DH : (head + 1) * DH, cols] = low_out
        product = low_out.astype(jnp.float32) * pair_ref[head, DH:, cols].astype(jnp.float32)
        stats_ref[heads + head : heads + head + 1, cols] = jnp.sum(product, axis=0, keepdims=True)
    stats_ref[:heads, :] = sums[...].T[:heads]
    stats_ref[2 * heads : 2 * heads + 1, :] = lower
    stats_ref[2 * heads + 1 : 2 * heads + 2, :] = upper
    stats_ref[2 * heads + 2 :, :] = jnp.zeros((STAT_ROWS - 2 * heads - 2, tokens), jnp.float32)


def stat_rows(stats_ref, heads, head):
    return stats_ref[head : head + 1, :], stats_ref[heads + head : heads + head + 1, :]


def span_bias(stats_ref, heads, first_block):
    lower, upper = stats_ref[2 * heads : 2 * heads + 1, :], stats_ref[2 * heads + 1 : 2 * heads + 2, :]
    return block_bias(first_block, lower, upper)


def query_side(place_ref, pair_ref, stats_ref, f0, f1, f2, f3, grad_ref):
    heads, _, tokens = pair_ref.shape
    slots = (f0, f1, f2, f3)
    span = f0.shape[2]
    bias = span_bias(stats_ref, heads, place_ref[0] - span // BLK)
    beside = [score_rows(span, s * (span // BLK)) for s in range(4)]
    above = dprob_rows(span)
    units = [(head, s) for head in range(heads) for s in range(4)]
    sides = {}

    def products(unit):
        head, s = units[unit]
        if s == 0:
            pair = pair_ref[head]
            logsum, delta = stat_rows(stats_ref, heads, head)
            sides[head] = score_side(pair, bias, logsum), dprob_side(pair, delta)
        left, grad_left = sides[head]
        raw = dot(left, jnp.concatenate([slots[s][head, :DH], beside[s]], axis=0), NN)
        return raw, dot(grad_left, jnp.concatenate([above, slots[s][head, DH:]], axis=0), NN)

    ahead = products(0)
    out = None
    for unit, (head, s) in enumerate(units):
        raw, dprob = ahead
        if unit + 1 < len(units):
            ahead = products(unit + 1)
        low = (jnp.exp2(raw * (LOG2E * FACTOR)) * dprob).astype(jnp.bfloat16)
        part = dot(slots[s][head, :DH], low, NT)
        out = part if s == 0 else out + part
        if s == 3:
            rows = slice(head * DH, (head + 1) * DH)
            grad_ref[rows, :] = (out * FACTOR).astype(jnp.bfloat16)


def frame_side(
    place_ref, own_ref, p0, p1, p2, p3, s0, s1, s2, s3, key_grad_ref, value_grad_ref
):
    heads, _, span = own_ref.shape
    sources = ((p0, s0), (p1, s1), (p2, s2), (p3, s3))
    bias = [span_bias(stats, heads, place_ref[0]) for _, stats in sources]
    beside = score_rows(span, 0)
    above = dprob_rows(span)
    units = [(head, j) for head in range(heads) for j in range(len(sources))]

    def products(unit):
        head, j = units[unit]
        right = jnp.concatenate([own_ref[head, :DH], beside], axis=0)
        grad_right = jnp.concatenate([above, own_ref[head, DH:]], axis=0)
        pair = sources[j][0][head]
        logsum, delta = stat_rows(sources[j][1], heads, head)
        raw = dot(score_side(pair, bias[j], logsum), right, NN)
        return raw, dot(dprob_side(pair, delta), grad_right, NN)

    ahead = products(0)
    key_out, value_out = None, None
    for unit, (head, j) in enumerate(units):
        raw, dprob = ahead
        if unit + 1 < len(units):
            ahead = products(unit + 1)
        pair_ref = sources[j][0]
        prob = jnp.exp2(raw * (LOG2E * FACTOR))
        key_part = dot(pair_ref[head, :DH], (prob * dprob).astype(jnp.bfloat16), NN)
        value_part = dot(pair_ref[head, DH:], prob.astype(jnp.bfloat16), NN)
        key_out = key_part if j == 0 else key_out + key_part
        value_out = value_part if j == 0 else value_out + value_part
        if j == len(sources) - 1:
            rows = slice(head * DH, (head + 1) * DH)
            key_grad_ref[rows, :] = (key_out * FACTOR).astype(jnp.bfloat16)
            value_grad_ref[rows, :] = value_out.astype(jnp.bfloat16)


def project(me_ref, weight_ref, attended_ref, kept_ref, sent_ref, whole):
    feats = attended_ref.shape[0]
    whole[...] = dot(weight_ref[...], attended_ref[...], NN)
    for place, flip in enumerate((0, 1)):
        block = pl.ds(pl.multiple_of((me_ref[0] ^ flip) * feats, feats), feats)
        kept_ref[place] = whole[block, :]
    for place, flip in enumerate((2, 3)):
        block = pl.ds(pl.multiple_of((me_ref[0] ^ flip) * feats, feats), feats)
        sent_ref[place] = whole[block, :].astype(jnp.bfloat16)


def after(value, *others):
    return lax.optimization_barrier((value,) + others)[0]


def call(kernel, outs, specs, *operands, scratch=(), steps=0):
    many = isinstance(outs, tuple)
    cost = pl.CostEstimate(flops=steps * 4_000_000_000, bytes_accessed=0, transcendentals=0)
    with jax.named_scope(kernel.__name__):
        return pl.pallas_call(
            kernel,
            out_shape=outs,
            in_specs=specs,
            out_specs=(VMEM,) * len(outs) if many else VMEM,
            scratch_shapes=scratch,
            compiler_params=PARAMS,
            cost_estimate=cost if steps else None,
        )(*operands)


def flipped(value, by):
    return lax.ppermute(value, "mp", [(i, i ^ by) for i in range(lax.axis_size("mp"))])


def on_device(queries, keys, values, out_weight, grad_out, alignment):
    queries, keys, values, grad_out = queries.T, keys.T, values.T, grad_out.T
    feats, frames = keys.shape
    tokens = queries.shape[1]
    heads = feats // DH
    me = lax.axis_index("mp").astype(jnp.int32).reshape(1)
    place = (lax.axis_index("seq").astype(jnp.int32) * (frames // BLK)).reshape(1)
    bf16, f32 = jnp.bfloat16, jnp.float32
    shape = jax.ShapeDtypeStruct

    grad_far = flipped(grad_out, 2)
    frame_pack = call(
        pack_frames,
        shape((heads, PAIR, frames), bf16),
        [HBM] * 2,
        keys,
        values,
        scratch=[pltpu.SemaphoreType.DMA((2, heads))],
    )
    grad_own = after(grad_out, frame_pack)
    grad_other = flipped(jnp.concatenate([grad_own, grad_far], axis=0), 1)
    later_pack = after(frame_pack, grad_far)
    window = [ring(later_pack, 1), frame_pack, ring(later_pack, -1), ring(frame_pack, -2)]

    token_pack = call(
        pack_tokens,
        shape((heads, PAIR, tokens), bf16),
        [SMEM] + [VMEM] * 5,
        me,
        grad_own,
        grad_far,
        grad_other,
        out_weight,
        queries,
        scratch=[pltpu.VMEM((4 * feats, tokens), bf16)],
    )
    turned_weight = after(out_weight, token_pack).T
    token_packs = [
        ring(token_pack, 1),
        ring(token_pack, -1),
        ring(after(token_pack, window[3]), 2),
    ]

    attended, stats = call(
        forward,
        (shape((feats, tokens), bf16), shape((STAT_ROWS, tokens), f32)),
        [SMEM] * 2 + [VMEM] * 5,
        place,
        after(alignment, turned_weight),
        token_pack,
        *window,
        scratch=[pltpu.VMEM((3, BLK, 4 * frames), f32), pltpu.VMEM((tokens, 128), f32)],
        steps=1,
    )
    sent_stats = after(stats, *token_packs)
    near_stats = [ring(sent_stats, 1), ring(sent_stats, -1), ring(sent_stats, 2)]

    kept, sent = call(
        project,
        (shape((2, feats, tokens), f32), shape((2, feats, tokens), bf16)),
        [SMEM] + [VMEM] * 2,
        me,
        turned_weight,
        attended,
        scratch=[pltpu.VMEM((4 * feats, tokens), f32)],
    )
    kept = kept + flipped(sent, 2).astype(f32)
    layer_output = (kept[0] + flipped(kept[1].astype(bf16), 1).astype(f32)).astype(bf16)
    query_grad = call(
        query_side,
        shape((feats, tokens), bf16),
        [SMEM] + [VMEM] * 6,
        place,
        token_pack,
        sent_stats,
        *window,
        steps=1,
    )
    key_grad, value_grad = call(
        frame_side,
        (shape((feats, frames), bf16),) * 2,
        [SMEM] + [VMEM] * 9,
        place,
        frame_pack,
        token_pack,
        *token_packs,
        after(sent_stats, layer_output, query_grad),
        *near_stats,
        steps=1,
    )
    return layer_output.T, query_grad.T, key_grad.T, value_grad.T


def solution(mesh):
    return jax.shard_map(
        on_device,
        mesh=mesh,
        in_specs=(
            P("seq", "mp"),
            P("seq", "mp"),
            P("seq", "mp"),
            P("mp", None),
            P("seq", "mp"),
            P("seq", None),
        ),
        out_specs=(P("seq", "mp"), P("seq", "mp"), P("seq", "mp"), P("seq", "mp")),
        check_vma=False,
    )
```

time: 157 us -> 84.1 us (0.54)
  the two profiles are of different devices: /device:TPU:27 before, /device:TPU:2 now
where the time goes in v2:
time: 84.1 us; the launch traced here: 83.9 us
  starting transfers between devices  44.5 us (53%)
  Pallas kernels  20.2 us (24%)
  waiting for transfers between devices  15 us (18%)
  local copies, waits for them, and re-layouts  2.61 us (3%)
    ppermute x9, starting transfers between devices, ring(): lax.ppermute(value, 'seq', [(i, (i + by) % count) for i in range(count)])  40.1 us
    pallas_call x6, Pallas kernels, call(): pl.pallas_call(kernel, out_shape=outs, in_specs=specs, out_specs=(VMEM,)...  20.2 us
    ppermute x9, waiting for transfers between devices, ring(): lax.ppermute(value, 'seq', [(i, (i + by) % count) for i in range(count)])  13.4 us
    ppermute x4, starting transfers between devices, flipped(): lax.ppermute(value, 'mp', [(i, i ^ by) for i in range(lax.axis_size('mp'))])  4.43 us
    unnamed x12, local copies, waits for them, and re-layouts  1.96 us
  transfers between devices with their start and end apart: 13, of which 4 were waited for; matrix products, arithmetic and copies ran while one was open for 2% of the time, Pallas kernels for 16%

profile of v2, /device:TPU:2, one launch (start us, length us, event | category | flops | bytes accessed | tf_op | source)
XLA Modules:
  0.0 83.9 jit_solution(5587293352807865113)
XLA Ops:
  0.6 2.4 %collective-permute-start = (bf16[320,256]{1,0:T(8,128)(2,1)}, bf16[320,256]{1,0:T(8,128)(2,1)S(1)}, u32[]{:S(2)}, u32[]{:S(2)}) collective-permute-start(bf16[320,256]{1,0:T(8,128)(2,1)} %bitcast.20), channel_id=1, source_target_pairs={{0,2},{1,3},{2,0},{3,1},{4,6},{5,7},{6,4},{7,5},{8,10},{9,11},{10,... | collective-permute-start | bytes 491528 | tf_op jit(solution)/shard_map/ppermute | solution.py:274
  3.0 1.0 %copy-done.2 = bf16[512,320]{0,1:T(8,128)(2,1)S(1)} copy-done((bf16[512,320]{0,1:T(8,128)(2,1)S(1)}, bf16[512,320]{0,1:T(8,128)(2,1)}, u32[]{:S(2)}) %copy-start.2) | copy-done | bytes 327704
  4.0 1.0 %copy-done.3 = bf16[512,320]{0,1:T(8,128)(2,1)S(1)} copy-done((bf16[512,320]{0,1:T(8,128)(2,1)S(1)}, bf16[512,320]{0,1:T(8,128)(2,1)}, u32[]{:S(2)}) %copy-start.3) | copy-done | bytes 327704
  4.9 0.9 %pack_frames.1.f1.own_ref = bf16[5,128,512]{2,1,0:T(8,128)(2,1)S(1)} custom-call(bf16[320,512]{1,0:T(8,128)(2,1)S(1)} %bitcast.23, bf16[320,512]{1,0:T(8,128)(2,1)S(1)} %bitcast.24), custom_call_target="tpu_custom_call" | custom-call | tf_op jit(solution)/shard_map/pack_frames/pallas_call | solution.py:262
  5.9 0.0 copy-start.4
  5.9 8.7 %collective-permute-start.4 = (bf16[5,128,512]{2,1,0:T(8,128)(2,1)S(1)}, bf16[5,128,512]{2,1,0:T(8,128)(2,1)S(1)}, u32[]{:S(2)}, u32[]{:S(2)}) collective-permute-start(bf16[5,128,512]{2,1,0:T(8,128)(2,1)S(1)} %pack_frames.1.f1.own_ref), channel_id=1, source_target_pairs={{0,248},{4,252},{8,0},{12,4},{16,8},{20,12},{24,16},{28,20},{32,24... | collective-permute-start | bytes 1966088 | tf_op jit(solution)/shard_map/ppermute | solution.py:27
  14.6 0.0 collective-permute-done.far_ref
  14.6 0.7 collective-permute-start.2
  15.3 7.1 %collective-permute-start.3 = (bf16[5,128,512]{2,1,0:T(8,128)(2,1)S(1)}, bf16[5,128,512]{2,1,0:T(8,128)(2,1)}, u32[]{:S(2)}, u32[]{:S(2)}) collective-permute-start(bf16[5,128,512]{2,1,0:T(8,128)(2,1)S(1)} %pack_frames.1.f1.own_ref), channel_id=1, source_target_pairs={{0,252},{4,0},{8,4},{12,8},{16,12},{20,16},{24,20},{28,24},{32,28}... | collective-permute-start | bytes 1966088 | tf_op jit(solution)/shard_map/ppermute | solution.py:27
  22.4 0.1 collective-permute-start.1
  22.5 1.6 %collective-permute-done.1.other_ref = bf16[640,256]{1,0:T(8,128)(2,1)S(1)} collective-permute-done((bf16[640,256]{1,0:T(8,128)(2,1)S(1)}, bf16[640,256]{1,0:T(8,128)(2,1)S(1)}, u32[]{:S(2)}, u32[]{:S(2)}) %collective-permute-start.1) | collective-permute-done | bytes 327712 | tf_op jit(solution)/shard_map/ppermute | solution.py:274
  24.1 0.4 pack_tokens.1.pair_ref.p0
  24.5 0.1 collective-permute-start.7
  24.6 7.7 %collective-permute-start.8 = (bf16[5,128,256]{2,1,0:T(8,128)(2,1)S(1)}, bf16[5,128,256]{2,1,0:T(8,128)(2,1)}, u32[]{:S(2)}, u32[]{:S(2)}) collective-permute-start(bf16[5,128,256]{2,1,0:T(8,128)(2,1)S(1)} %pack_tokens.1.pair_ref.p0), channel_id=1, source_target_pairs={{0,252},{4,0},{8,4},{12,8},{16,12},{20,16},{24,20},{28,24},{32,28}... | collective-permute-start | bytes 983048 | tf_op jit(solution)/shard_map/ppermute | solution.py:27
  32.3 0.6 copy.10
  33.0 0.0 copy-start.5
  33.0 0.1 collective-permute-start.9
  33.1 6.5 %collective-permute-done.2.f0 = bf16[5,128,512]{2,1,0:T(8,128)(2,1)} collective-permute-done((bf16[5,128,512]{2,1,0:T(8,128)(2,1)S(1)}, bf16[5,128,512]{2,1,0:T(8,128)(2,1)}, u32[]{:S(2)}, u32[]{:S(2)}) %collective-permute-start.2) | collective-permute-done | bytes 655392 | tf_op jit(solution)/shard_map/ppermute | solution.py:27
  39.6 4.3 %collective-permute-done.3.f2 = bf16[5,128,512]{2,1,0:T(8,128)(2,1)} collective-permute-done((bf16[5,128,512]{2,1,0:T(8,128)(2,1)S(1)}, bf16[5,128,512]{2,1,0:T(8,128)(2,1)}, u32[]{:S(2)}, u32[]{:S(2)}) %collective-permute-start.3) | collective-permute-done | bytes 655392 | tf_op jit(solution)/shard_map/ppermute | solution.py:27
  43.8 5.4 %forward.1 = (bf16[320,256]{1,0:T(8,128)(2,1)S(1)}, f32[16,256]{1,0:T(8,128)S(1)}) custom-call(s32[1]{0:T(128)} %bitcast.6.place_ref, s32[2,2]{1,0:T(2,128)S(1)} %copy-done.5, bf16[5,128,256]{2,1,0:T(8,128)(2,1)S(1)} %pack_tokens.1.pair_ref.p0, bf16[5,128,512]{2,1,0:T(8,128)(2,1)} %collective-permute-done.2.f0, ...), custom_call_target="tpu_custom_call" | custom-call | flops 4000000000 | tf_op jit(solution)/shard_map/forward/pallas_call | solution.py:262
  49.2 0.6 project.1
  49.8 1.9 %collective-permute-start.5 = (bf16[2,320,256]{2,1,0:T(8,128)(2,1)S(1)}, bf16[2,320,256]{2,1,0:T(8,128)(2,1)S(1)}, u32[]{:S(2)}, u32[]{:S(2)}) collective-permute-start(bf16[2,320,256]{2,1,0:T(8,128)(2,1)S(1)} %get-tuple-element.23), channel_id=1, source_target_pairs={{0,2},{1,3},{2,0},{3,1},{4,6},{5,7},{6,4},{7,5},{8,10},{9,11},{10,... | collective-permute-start | bytes 983048 | tf_op jit(solution)/shard_map/ppermute | solution.py:274
  51.7 0.0 collective-permute-done.7.p1
  51.7 0.0 collective-permute-done.9.p3
  51.7 1.7 %collective-permute-start.10 = (f32[16,256]{1,0:T(8,128)S(1)}, f32[16,256]{1,0:T(8,128)S(1)}, u32[]{:S(2)}, u32[]{:S(2)}) collective-permute-start(f32[16,256]{1,0:T(8,128)S(1)} %get-tuple-element.27.stats_ref.s0), channel_id=1, source_target_pairs={{0,4},{4,8},{8,12},{12,16},{16,20},{20,24},{24,28},{28,32},{32,36}... | collective-permute-start | bytes 49160 | tf_op jit(solution)/shard_map/ppermute | solution.py:27
  53.5 14.0 %collective-permute-start.11 = (f32[16,256]{1,0:T(8,128)S(1)}, f32[16,256]{1,0:T(8,128)S(1)}, u32[]{:S(2)}, u32[]{:S(2)}) collective-permute-start(f32[16,256]{1,0:T(8,128)S(1)} %get-tuple-element.27.stats_ref.s0), channel_id=1, source_target_pairs={{0,252},{4,0},{8,4},{12,8},{16,12},{20,16},{24,20},{28,24},{32,28}... | collective-permute-start | bytes 49160 | tf_op jit(solution)/shard_map/ppermute | solution.py:27
  67.5 0.1 convert_add_fusion
  67.6 0.1 collective-permute-start.6
  67.7 6.2 %query_side.1 = bf16[320,256]{1,0:T(8,128)(2,1)} custom-call(s32[1]{0:T(128)} %bitcast.6.place_ref, bf16[5,128,256]{2,1,0:T(8,128)(2,1)S(1)} %pack_tokens.1.pair_ref.p0, f32[16,256]{1,0:T(8,128)S(1)} %get-tuple-element.27.stats_ref.s0, bf16[5,128,512]{2,1,0:T(8,128)(2,1)} %collective-permute-done.2.f0, bf16[5,128,512]{2,1,0:T(8,128)(2,1)S(1)} %pack_frames.1.f1.own_ref, ...), custom_call_target="tpu_custom_call" | custom-call | flops 4000000000 | tf_op jit(solution)/shard_map/query_side/pallas_call | solution.py:262
  73.9 0.7 fusion.1
  74.7 2.6 %collective-permute-done.12.s3 = f32[16,256]{1,0:T(8,128)S(1)} collective-permute-done((f32[16,256]{1,0:T(8,128)S(1)}, f32[16,256]{1,0:T(8,128)S(1)}, u32[]{:S(2)}, u32[]{:S(2)}) %collective-permute-start.12) | collective-permute-done | bytes 16416 | tf_op jit(solution)/shard_map/ppermute | solution.py:27
  77.3 6.6 %frame_side.1 = (bf16[320,512]{1,0:T(8,128)(2,1)}, bf16[320,512]{1,0:T(8,128)(2,1)}) custom-call(s32[1]{0:T(128)} %bitcast.6.place_ref, bf16[5,128,512]{2,1,0:T(8,128)(2,1)S(1)} %pack_frames.1.f1.own_ref, bf16[5,128,256]{2,1,0:T(8,128)(2,1)S(1)} %pack_tokens.1.pair_ref.p0, bf16[5,128,256]{2,1,0:T(8,128)(2,1)} %collective-permute-done.7.p1, ...), custom_call_target="tpu_custom_call" | custom-call | flops 4000000000 | tf_op jit(solution)/shard_map/frame_side/pallas_call | solution.py:262
  (17 shorter events, 0.1 us)
Async XLA Ops:
  0.6 13.9 %collective-permute-start = (bf16[320,256]{1,0:T(8,128)(2,1)}, bf16[320,256]{1,0:T(8,128)(2,1)S(1)}, u32[]{:S(2)}, u32[]{:S(2)}) collective-permute-start(bf16[320,256]{1,0:T(8,128)(2,1)} %bitcast.20), channel_id=1, source_target_pairs={{0,2},{1,3},{2,0},{3,1},{4,6},{5,7},{6,4},{7,5},{8,10},{9,11},{10,... | collective-permute-start | bytes 491528 | tf_op jit(solution)/shard_map/ppermute | solution.py:274
  3.0 1.0 %copy-start.2 = (bf16[512,320]{0,1:T(8,128)(2,1)S(1)}, bf16[512,320]{0,1:T(8,128)(2,1)}, u32[]{:S(2)}) copy-start(bf16[512,320]{0,1:T(8,128)(2,1)} %param.7) | copy-start | bytes 983044
  4.0 1.0 %copy-start.3 = (bf16[512,320]{0,1:T(8,128)(2,1)S(1)}, bf16[512,320]{0,1:T(8,128)(2,1)}, u32[]{:S(2)}) copy-start(bf16[512,320]{0,1:T(8,128)(2,1)} %param.8) | copy-start | bytes 983044
  4.9 17.4 %copy-start.1 = (bf16[256,320]{0,1:T(8,128)(2,1)S(1)}, bf16[256,320]{0,1:T(8,128)(2,1)}, u32[]{:S(2)}) copy-start(bf16[256,320]{0,1:T(8,128)(2,1)} %param.10) | copy-start | bytes 491524
  4.9 19.1 %copy-start = (bf16[320,1280]{1,0:T(8,128)(2,1)S(1)}, bf16[320,1280]{1,0:T(8,128)(2,1)}, u32[]{:S(2)}) copy-start(bf16[320,1280]{1,0:T(8,128)(2,1)} %weight_ref.1) | copy-start | bytes 2457604
  5.9 18.2 %copy-start.4 = (bf16[256,320]{0,1:T(8,128)(2,1)S(1)}, bf16[256,320]{0,1:T(8,128)(2,1)}, u32[]{:S(2)}) copy-start(bf16[256,320]{0,1:T(8,128)(2,1)} %param.6) | copy-start | bytes 491524
  5.9 27.1 %collective-permute-start.4 = (bf16[5,128,512]{2,1,0:T(8,128)(2,1)S(1)}, bf16[5,128,512]{2,1,0:T(8,128)(2,1)S(1)}, u32[]{:S(2)}, u32[]{:S(2)}) collective-permute-start(bf16[5,128,512]{2,1,0:T(8,128)(2,1)S(1)} %pack_frames.1.f1.own_ref), channel_id=1, source_target_pairs={{0,248},{4,252},{8,0},{12,4},{16,8},{20,12},{24,16},{28,20},{32,24... | collective-permute-start | bytes 1966088 | tf_op jit(solution)/shard_map/ppermute | solution.py:27
  14.6 25.0 %collective-permute-start.2 = (bf16[5,128,512]{2,1,0:T(8,128)(2,1)S(1)}, bf16[5,128,512]{2,1,0:T(8,128)(2,1)}, u32[]{:S(2)}, u32[]{:S(2)}) collective-permute-start(bf16[5,128,512]{2,1,0:T(8,128)(2,1)S(1)} %pack_frames.1.f1.own_ref), channel_id=1, source_target_pairs={{0,4},{4,8},{8,12},{12,16},{16,20},{20,24},{24,28},{28,32},{32,36}... | collective-permute-start | bytes 1966088 | tf_op jit(solution)/shard_map/ppermute | solution.py:27
  15.3 28.6 %collective-permute-start.3 = (bf16[5,128,512]{2,1,0:T(8,128)(2,1)S(1)}, bf16[5,128,512]{2,1,0:T(8,128)(2,1)}, u32[]{:S(2)}, u32[]{:S(2)}) collective-permute-start(bf16[5,128,512]{2,1,0:T(8,128)(2,1)S(1)} %pack_frames.1.f1.own_ref), channel_id=1, source_target_pairs={{0,252},{4,0},{8,4},{12,8},{16,12},{20,16},{24,20},{28,24},{32,28}... | collective-permute-start | bytes 1966088 | tf_op jit(solution)/shard_map/ppermute | solution.py:27
  22.4 1.7 %collective-permute-start.1 = (bf16[640,256]{1,0:T(8,128)(2,1)S(1)}, bf16[640,256]{1,0:T(8,128)(2,1)S(1)}, u32[]{:S(2)}, u32[]{:S(2)}) collective-permute-start(bf16[640,256]{1,0:T(8,128)(2,1)S(1)} %pad_maximum_fusion), channel_id=1, source_target_pairs={{0,1},{1,0},{2,3},{3,2},{4,5},{5,4},{6,7},{7,6},{8,9},{9,8},{10,11... | collective-permute-start | bytes 983048 | tf_op jit(solution)/shard_map/ppermute | solution.py:274
  24.5 27.2 %collective-permute-start.7 = (bf16[5,128,256]{2,1,0:T(8,128)(2,1)S(1)}, bf16[5,128,256]{2,1,0:T(8,128)(2,1)}, u32[]{:S(2)}, u32[]{:S(2)}) collective-permute-start(bf16[5,128,256]{2,1,0:T(8,128)(2,1)S(1)} %pack_tokens.1.pair_ref.p0), channel_id=1, source_target_pairs={{0,4},{4,8},{8,12},{12,16},{16,20},{20,24},{24,28},{28,32},{32,36}... | collective-permute-start | bytes 983048 | tf_op jit(solution)/shard_map/ppermute | solution.py:27
  24.6 27.1 %collective-permute-start.8 = (bf16[5,128,256]{2,1,0:T(8,128)(2,1)S(1)}, bf16[5,128,256]{2,1,0:T(8,128)(2,1)}, u32[]{:S(2)}, u32[]{:S(2)}) collective-permute-start(bf16[5,128,256]{2,1,0:T(8,128)(2,1)S(1)} %pack_tokens.1.pair_ref.p0), channel_id=1, source_target_pairs={{0,252},{4,0},{8,4},{12,8},{16,12},{20,16},{24,20},{28,24},{32,28}... | collective-permute-start | bytes 983048 | tf_op jit(solution)/shard_map/ppermute | solution.py:27
  33.0 10.9 %copy-start.5 = (s32[2,2]{1,0:T(2,128)S(1)}, s32[2,2]{1,0:T(2,128)}, u32[]{:S(2)}) copy-start(s32[2,2]{1,0:T(2,128)} %align_ref) | copy-start | bytes 52
  33.0 18.7 %collective-permute-start.9 = (bf16[5,128,256]{2,1,0:T(8,128)(2,1)S(1)}, bf16[5,128,256]{2,1,0:T(8,128)(2,1)S(1)}, u32[]{:S(2)}, u32[]{:S(2)}) collective-permute-start(bf16[5,128,256]{2,1,0:T(8,128)(2,1)S(1)} %pack_tokens.1.pair_ref.p0), channel_id=1, source_target_pairs={{0,8},{4,12},{8,16},{12,20},{16,24},{20,28},{24,32},{28,36},{32,40... | collective-permute-start | bytes 983048 | tf_op jit(solution)/shard_map/ppermute | solution.py:27
  49.8 17.7 %collective-permute-start.5 = (bf16[2,320,256]{2,1,0:T(8,128)(2,1)S(1)}, bf16[2,320,256]{2,1,0:T(8,128)(2,1)S(1)}, u32[]{:S(2)}, u32[]{:S(2)}) collective-permute-start(bf16[2,320,256]{2,1,0:T(8,128)(2,1)S(1)} %get-tuple-element.23), channel_id=1, source_target_pairs={{0,2},{1,3},{2,0},{3,1},{4,6},{5,7},{6,4},{7,5},{8,10},{9,11},{10,... | collective-permute-start | bytes 983048 | tf_op jit(solution)/shard_map/ppermute | solution.py:274
  51.7 22.9 %collective-permute-start.10 = (f32[16,256]{1,0:T(8,128)S(1)}, f32[16,256]{1,0:T(8,128)S(1)}, u32[]{:S(2)}, u32[]{:S(2)}) collective-permute-start(f32[16,256]{1,0:T(8,128)S(1)} %get-tuple-element.27.stats_ref.s0), channel_id=1, source_target_pairs={{0,4},{4,8},{8,12},{12,16},{16,20},{20,24},{24,28},{28,32},{32,36}... | collective-permute-start | bytes 49160 | tf_op jit(solution)/shard_map/ppermute | solution.py:27
  53.5 21.2 %collective-permute-start.11 = (f32[16,256]{1,0:T(8,128)S(1)}, f32[16,256]{1,0:T(8,128)S(1)}, u32[]{:S(2)}, u32[]{:S(2)}) collective-permute-start(f32[16,256]{1,0:T(8,128)S(1)} %get-tuple-element.27.stats_ref.s0), channel_id=1, source_target_pairs={{0,252},{4,0},{8,4},{12,8},{16,12},{20,16},{24,20},{28,24},{32,28}... | collective-permute-start | bytes 49160 | tf_op jit(solution)/shard_map/ppermute | solution.py:27
  67.5 9.8 %collective-permute-start.12 = (f32[16,256]{1,0:T(8,128)S(1)}, f32[16,256]{1,0:T(8,128)S(1)}, u32[]{:S(2)}, u32[]{:S(2)}) collective-permute-start(f32[16,256]{1,0:T(8,128)S(1)} %get-tuple-element.27.stats_ref.s0), channel_id=1, source_target_pairs={{0,8},{4,12},{8,16},{12,20},{16,24},{20,28},{24,32},{28,36},{32,40... | collective-permute-start | bytes 49160 | tf_op jit(solution)/shard_map/ppermute | solution.py:27
  67.6 6.3 %collective-permute-start.6 = (bf16[320,256]{1,0:T(8,128)(2,1)S(1)}, bf16[320,256]{1,0:T(8,128)(2,1)S(1)}, u32[]{:S(2)}, u32[]{:S(2)}) collective-permute-start(bf16[320,256]{1,0:T(8,128)(2,1)S(1)} %fusion.2), channel_id=1, source_target_pairs={{0,1},{1,0},{2,3},{3,2},{4,5},{5,4},{6,7},{7,6},{8,9},{9,8},{10,11... | collective-permute-start | bytes 491528 | tf_op jit(solution)/shard_map/ppermute | solution.py:274

commit v3 on v2

--- a/solution.py
+++ b/solution.py
@@ -311,11 +311,9 @@
         scratch=[pltpu.VMEM((4 * feats, tokens), bf16)],
     )
     turned_weight = after(out_weight, token_pack).T
-    token_packs = [
-        ring(token_pack, 1),
-        ring(token_pack, -1),
-        ring(after(token_pack, window[3]), 2),
-    ]
+    sent_pack = after(token_pack, window[3])
+    late_pack = after(token_pack, *window)
+    token_packs = [ring(late_pack, 1), ring(sent_pack, -1), ring(late_pack, 2)]
 
     attended, stats = call(
         forward,
@@ -328,7 +326,7 @@
         scratch=[pltpu.VMEM((3, BLK, 4 * frames), f32), pltpu.VMEM((tokens, 128), f32)],
         steps=1,
     )
-    sent_stats = after(stats, *token_packs)
+    sent_stats = after(stats, token_packs[1])
     near_stats = [ring(sent_stats, 1), ring(sent_stats, -1), ring(sent_stats, 2)]
 
     kept, sent = call(
@@ -337,7 +335,7 @@
         [SMEM] + [VMEM] * 2,
         me,
         turned_weight,
-        attended,
+        after(attended, near_stats[0]),
         scratch=[pltpu.VMEM((4 * feats, tokens), f32)],
     )
     kept = kept + flipped(sent, 2).astype(f32)
@@ -348,7 +346,7 @@
         [SMEM] + [VMEM] * 6,
         place,
         token_pack,
-        sent_stats,
+        after(sent_stats, token_packs[0]),
         *window,
         steps=1,
     )
@@ -360,7 +358,7 @@
         frame_pack,
         token_pack,
         *token_packs,
-        after(sent_stats, layer_output, query_grad),
+        after(sent_stats, query_grad),
         *near_stats,
         steps=1,
     )

time: 84.1 us -> 78.7 us (0.936)
  the two profiles are of different devices: /device:TPU:2 before, /device:TPU:113 now
where the time goes in v3:
time: 78.7 us; the launch traced here: 78.5 us
  waiting for transfers between devices  30.9 us (39%)
  starting transfers between devices  24.4 us (31%)
  Pallas kernels  19.1 us (24%)
  local copies, waits for them, and re-layouts  2.62 us (3%)
  other arithmetic  0.8 us (1%)
    ppermute x9, waiting for transfers between devices, ring(): lax.ppermute(value, 'seq', [(i, (i + by) % count) for i in range(count)])  28.6 us
    pallas_call x6, Pallas kernels, call(): pl.pallas_call(kernel, out_shape=outs, in_specs=specs, out_specs=(VMEM,)...  19.1 us
    ppermute x9, starting transfers between devices, ring(): lax.ppermute(value, 'seq', [(i, (i + by) % count) for i in range(count)])  16.6 us
    ppermute x4, starting transfers between devices, flipped(): lax.ppermute(value, 'mp', [(i, i ^ by) for i in range(lax.axis_size('mp'))])  7.79 us
    ppermute x4, waiting for transfers between devices, flipped(): lax.ppermute(value, 'mp', [(i, i ^ by) for i in range(lax.axis_size('mp'))])  2.29 us
    unnamed x12, local copies, waits for them, and re-layouts  1.96 us
  transfers between devices with their start and end apart: 13, of which 4 were waited for; matrix products, arithmetic and copies ran while one was open for 1% of the time, Pallas kernels for 24%

profile of v3, /device:TPU:113, one launch (start us, length us, event | category | flops | bytes accessed | tf_op | source)
XLA Modules:
  0.0 78.5 jit_solution(1990527654463775820)
XLA Ops:
  0.6 1.3 %collective-permute-start = (bf16[320,256]{1,0:T(8,128)(2,1)}, bf16[320,256]{1,0:T(8,128)(2,1)S(1)}, u32[]{:S(2)}, u32[]{:S(2)}) collective-permute-start(bf16[320,256]{1,0:T(8,128)(2,1)} %bitcast.23), channel_id=1, source_target_pairs={{0,2},{1,3},{2,0},{3,1},{4,6},{5,7},{6,4},{7,5},{8,10},{9,11},{10,... | collective-permute-start | bytes 491528 | tf_op jit(solution)/shard_map/ppermute | solution.py:274
  1.9 1.0 %copy-done.2 = bf16[512,320]{0,1:T(8,128)(2,1)S(1)} copy-done((bf16[512,320]{0,1:T(8,128)(2,1)S(1)}, bf16[512,320]{0,1:T(8,128)(2,1)}, u32[]{:S(2)}) %copy-start.2) | copy-done | bytes 327704
  2.9 1.0 %copy-done.3 = bf16[512,320]{0,1:T(8,128)(2,1)S(1)} copy-done((bf16[512,320]{0,1:T(8,128)(2,1)S(1)}, bf16[512,320]{0,1:T(8,128)(2,1)}, u32[]{:S(2)}) %copy-start.3) | copy-done | bytes 327704
  3.9 0.9 %pack_frames.1.f1.own_ref = bf16[5,128,512]{2,1,0:T(8,128)(2,1)S(1)} custom-call(bf16[320,512]{1,0:T(8,128)(2,1)S(1)} %bitcast.26, bf16[320,512]{1,0:T(8,128)(2,1)S(1)} %bitcast.27), custom_call_target="tpu_custom_call" | custom-call | tf_op jit(solution)/shard_map/pack_frames/pallas_call | solution.py:262
  4.8 0.0 copy-start.4
  4.8 0.1 collective-permute-start.4
  5.0 1.0 %collective-permute-done.far_ref = bf16[320,256]{1,0:T(8,128)(2,1)S(1)} collective-permute-done((bf16[320,256]{1,0:T(8,128)(2,1)}, bf16[320,256]{1,0:T(8,128)(2,1)S(1)}, u32[]{:S(2)}, u32[]{:S(2)}) %collective-permute-start) | collective-permute-done | bytes 163872 | tf_op jit(solution)/shard_map/ppermute | solution.py:274
  6.0 1.0 %collective-permute-start.2 = (bf16[5,128,512]{2,1,0:T(8,128)(2,1)S(1)}, bf16[5,128,512]{2,1,0:T(8,128)(2,1)}, u32[]{:S(2)}, u32[]{:S(2)}) collective-permute-start(bf16[5,128,512]{2,1,0:T(8,128)(2,1)S(1)} %pack_frames.1.f1.own_ref), channel_id=1, source_target_pairs={{0,4},{4,8},{8,12},{12,16},{16,20},{20,24},{24,28},{28,32},{32,36}... | collective-permute-start | bytes 1966088 | tf_op jit(solution)/shard_map/ppermute | solution.py:27
  7.0 0.5 collective-permute-start.3
  7.5 2.2 %collective-permute-start.1 = (bf16[640,256]{1,0:T(8,128)(2,1)S(1)}, bf16[640,256]{1,0:T(8,128)(2,1)S(1)}, u32[]{:S(2)}, u32[]{:S(2)}) collective-permute-start(bf16[640,256]{1,0:T(8,128)(2,1)S(1)} %pad_maximum_fusion), channel_id=1, source_target_pairs={{0,1},{1,0},{2,3},{3,2},{4,5},{5,4},{6,7},{7,6},{8,9},{9,8},{10,11... | collective-permute-start | bytes 983048 | tf_op jit(solution)/shard_map/ppermute | solution.py:274
  9.7 1.3 %collective-permute-done.1.other_ref = bf16[640,256]{1,0:T(8,128)(2,1)S(1)} collective-permute-done((bf16[640,256]{1,0:T(8,128)(2,1)S(1)}, bf16[640,256]{1,0:T(8,128)(2,1)S(1)}, u32[]{:S(2)}, u32[]{:S(2)}) %collective-permute-start.1) | collective-permute-done | bytes 327712 | tf_op jit(solution)/shard_map/ppermute | solution.py:274
  10.9 0.4 pack_tokens.1.pair_ref.p0
  11.4 0.6 copy.10
  12.0 0.0 copy-start.5
  12.0 14.5 %collective-permute-done.4.f3 = bf16[5,128,512]{2,1,0:T(8,128)(2,1)S(1)} collective-permute-done((bf16[5,128,512]{2,1,0:T(8,128)(2,1)S(1)}, bf16[5,128,512]{2,1,0:T(8,128)(2,1)S(1)}, u32[]{:S(2)}, u32[]{:S(2)}) %collective-permute-start.4) | collective-permute-done | bytes 655392 | tf_op jit(solution)/shard_map/ppermute | solution.py:27
  26.5 0.0 collective-permute-start.5
  26.5 14.0 %collective-permute-done.2.f0 = bf16[5,128,512]{2,1,0:T(8,128)(2,1)} collective-permute-done((bf16[5,128,512]{2,1,0:T(8,128)(2,1)S(1)}, bf16[5,128,512]{2,1,0:T(8,128)(2,1)}, u32[]{:S(2)}, u32[]{:S(2)}) %collective-permute-start.2) | collective-permute-done | bytes 655392 | tf_op jit(solution)/shard_map/ppermute | solution.py:27
  40.6 0.0 collective-permute-done.3.f2
  40.6 2.3 %collective-permute-start.9 = (bf16[5,128,256]{2,1,0:T(8,128)(2,1)S(1)}, bf16[5,128,256]{2,1,0:T(8,128)(2,1)S(1)}, u32[]{:S(2)}, u32[]{:S(2)}) collective-permute-start(bf16[5,128,256]{2,1,0:T(8,128)(2,1)S(1)} %pack_tokens.1.pair_ref.p0), channel_id=1, source_target_pairs={{0,4},{4,8},{8,12},{12,16},{16,20},{20,24},{24,28},{28,32},{32,36}... | collective-permute-start | bytes 983048 | tf_op jit(solution)/shard_map/ppermute | solution.py:27
  42.9 5.4 %forward.1 = (bf16[320,256]{1,0:T(8,128)(2,1)S(1)}, f32[16,256]{1,0:T(8,128)S(1)}) custom-call(s32[1]{0:T(128)} %bitcast.6.place_ref, s32[2,2]{1,0:T(2,128)S(1)} %copy-done.5, bf16[5,128,256]{2,1,0:T(8,128)(2,1)S(1)} %pack_tokens.1.pair_ref.p0, bf16[5,128,512]{2,1,0:T(8,128)(2,1)} %collective-permute-done.2.f0, ...), custom_call_target="tpu_custom_call" | custom-call | flops 4000000000 | tf_op jit(solution)/shard_map/forward/pallas_call | solution.py:262
  48.3 0.1 collective-permute-start.6
  48.4 5.8 %collective-permute-start.10 = (bf16[5,128,256]{2,1,0:T(8,128)(2,1)S(1)}, bf16[5,128,256]{2,1,0:T(8,128)(2,1)S(1)}, u32[]{:S(2)}, u32[]{:S(2)}) collective-permute-start(bf16[5,128,256]{2,1,0:T(8,128)(2,1)S(1)} %pack_tokens.1.pair_ref.p0), channel_id=1, source_target_pairs={{0,8},{4,12},{8,16},{12,20},{16,24},{20,28},{24,32},{28,36},{32,40... | collective-permute-start | bytes 983048 | tf_op jit(solution)/shard_map/ppermute | solution.py:27
  54.2 6.8 %collective-permute-start.12 = (f32[16,256]{1,0:T(8,128)S(1)}, f32[16,256]{1,0:T(8,128)S(1)}, u32[]{:S(2)}, u32[]{:S(2)}) collective-permute-start(f32[16,256]{1,0:T(8,128)S(1)} %get-tuple-element.33.stats_ref.s0), channel_id=1, source_target_pairs={{0,8},{4,12},{8,16},{12,20},{16,24},{20,28},{24,32},{28,36},{32,40... | collective-permute-start | bytes 49160 | tf_op jit(solution)/shard_map/ppermute | solution.py:27
  61.0 0.0 collective-permute-done.6.s1
  61.0 0.6 project.1
  61.6 0.3 collective-permute-start.7
  62.0 0.0 collective-permute-done.9.p1
  62.0 6.2 %query_side.1 = bf16[320,256]{1,0:T(8,128)(2,1)} custom-call(s32[1]{0:T(128)} %bitcast.6.place_ref, bf16[5,128,256]{2,1,0:T(8,128)(2,1)S(1)} %pack_tokens.1.pair_ref.p0, f32[16,256]{1,0:T(8,128)S(1)} %get-tuple-element.33.stats_ref.s0, bf16[5,128,512]{2,1,0:T(8,128)(2,1)} %collective-permute-done.2.f0, bf16[5,128,512]{2,1,0:T(8,128)(2,1)S(1)} %pack_frames.1.f1.own_ref, ...), custom_call_target="tpu_custom_call" | custom-call | flops 4000000000 | tf_op jit(solution)/shard_map/query_side/pallas_call | solution.py:262
  68.2 0.1 convert_add_fusion
  68.3 4.0 %collective-permute-start.8 = (bf16[320,256]{1,0:T(8,128)(2,1)S(1)}, bf16[320,256]{1,0:T(8,128)(2,1)S(1)}, u32[]{:S(2)}, u32[]{:S(2)}) collective-permute-start(bf16[320,256]{1,0:T(8,128)(2,1)S(1)} %fusion.3), channel_id=1, source_target_pairs={{0,1},{1,0},{2,3},{3,2},{4,5},{5,4},{6,7},{7,6},{8,9},{9,8},{10,11... | collective-permute-start | bytes 491528 | tf_op jit(solution)/shard_map/ppermute | solution.py:274
  72.3 5.5 %frame_side.1 = (bf16[320,512]{1,0:T(8,128)(2,1)}, bf16[320,512]{1,0:T(8,128)(2,1)}) custom-call(s32[1]{0:T(128)} %bitcast.6.place_ref, bf16[5,128,512]{2,1,0:T(8,128)(2,1)S(1)} %pack_frames.1.f1.own_ref, bf16[5,128,256]{2,1,0:T(8,128)(2,1)S(1)} %pack_tokens.1.pair_ref.p0, bf16[5,128,256]{2,1,0:T(8,128)(2,1)S(1)} %collective-permute-done.9.p1, ...), custom_call_target="tpu_custom_call" | custom-call | flops 4000000000 | tf_op jit(solution)/shard_map/frame_side/pallas_call | solution.py:262
  77.8 0.7 fusion.2
  (17 shorter events, 0.1 us)
Async XLA Ops:
  0.6 5.4 %collective-permute-start = (bf16[320,256]{1,0:T(8,128)(2,1)}, bf16[320,256]{1,0:T(8,128)(2,1)S(1)}, u32[]{:S(2)}, u32[]{:S(2)}) collective-permute-start(bf16[320,256]{1,0:T(8,128)(2,1)} %bitcast.23), channel_id=1, source_target_pairs={{0,2},{1,3},{2,0},{3,1},{4,6},{5,7},{6,4},{7,5},{8,10},{9,11},{10,... | collective-permute-start | bytes 491528 | tf_op jit(solution)/shard_map/ppermute | solution.py:274
  1.9 1.0 %copy-start.2 = (bf16[512,320]{0,1:T(8,128)(2,1)S(1)}, bf16[512,320]{0,1:T(8,128)(2,1)}, u32[]{:S(2)}) copy-start(bf16[512,320]{0,1:T(8,128)(2,1)} %param.7) | copy-start | bytes 983044
  2.9 1.0 %copy-start.3 = (bf16[512,320]{0,1:T(8,128)(2,1)S(1)}, bf16[512,320]{0,1:T(8,128)(2,1)}, u32[]{:S(2)}) copy-start(bf16[512,320]{0,1:T(8,128)(2,1)} %param.8) | copy-start | bytes 983044
  3.9 3.6 %copy-start.1 = (bf16[256,320]{0,1:T(8,128)(2,1)S(1)}, bf16[256,320]{0,1:T(8,128)(2,1)}, u32[]{:S(2)}) copy-start(bf16[256,320]{0,1:T(8,128)(2,1)} %param.10) | copy-start | bytes 491524
  3.9 7.1 %copy-start = (bf16[320,1280]{1,0:T(8,128)(2,1)S(1)}, bf16[320,1280]{1,0:T(8,128)(2,1)}, u32[]{:S(2)}) copy-start(bf16[320,1280]{1,0:T(8,128)(2,1)} %weight_ref.1) | copy-start | bytes 2457604
  4.8 6.1 %copy-start.4 = (bf16[256,320]{0,1:T(8,128)(2,1)S(1)}, bf16[256,320]{0,1:T(8,128)(2,1)}, u32[]{:S(2)}) copy-start(bf16[256,320]{0,1:T(8,128)(2,1)} %param.6) | copy-start | bytes 491524
  4.8 21.7 %collective-permute-start.4 = (bf16[5,128,512]{2,1,0:T(8,128)(2,1)S(1)}, bf16[5,128,512]{2,1,0:T(8,128)(2,1)S(1)}, u32[]{:S(2)}, u32[]{:S(2)}) collective-permute-start(bf16[5,128,512]{2,1,0:T(8,128)(2,1)S(1)} %pack_frames.1.f1.own_ref), channel_id=1, source_target_pairs={{0,248},{4,252},{8,0},{12,4},{16,8},{20,12},{24,16},{28,20},{32,24... | collective-permute-start | bytes 1966088 | tf_op jit(solution)/shard_map/ppermute | solution.py:27
  6.0 34.6 %collective-permute-start.2 = (bf16[5,128,512]{2,1,0:T(8,128)(2,1)S(1)}, bf16[5,128,512]{2,1,0:T(8,128)(2,1)}, u32[]{:S(2)}, u32[]{:S(2)}) collective-permute-start(bf16[5,128,512]{2,1,0:T(8,128)(2,1)S(1)} %pack_frames.1.f1.own_ref), channel_id=1, source_target_pairs={{0,4},{4,8},{8,12},{12,16},{16,20},{20,24},{24,28},{28,32},{32,36}... | collective-permute-start | bytes 1966088 | tf_op jit(solution)/shard_map/ppermute | solution.py:27
  7.0 33.6 %collective-permute-start.3 = (bf16[5,128,512]{2,1,0:T(8,128)(2,1)S(1)}, bf16[5,128,512]{2,1,0:T(8,128)(2,1)}, u32[]{:S(2)}, u32[]{:S(2)}) collective-permute-start(bf16[5,128,512]{2,1,0:T(8,128)(2,1)S(1)} %pack_frames.1.f1.own_ref), channel_id=1, source_target_pairs={{0,252},{4,0},{8,4},{12,8},{16,12},{20,16},{24,20},{28,24},{32,28}... | collective-permute-start | bytes 1966088 | tf_op jit(solution)/shard_map/ppermute | solution.py:27
  7.5 3.4 %collective-permute-start.1 = (bf16[640,256]{1,0:T(8,128)(2,1)S(1)}, bf16[640,256]{1,0:T(8,128)(2,1)S(1)}, u32[]{:S(2)}, u32[]{:S(2)}) collective-permute-start(bf16[640,256]{1,0:T(8,128)(2,1)S(1)} %pad_maximum_fusion), channel_id=1, source_target_pairs={{0,1},{1,0},{2,3},{3,2},{4,5},{5,4},{6,7},{7,6},{8,9},{9,8},{10,11... | collective-permute-start | bytes 983048 | tf_op jit(solution)/shard_map/ppermute | solution.py:274
  12.0 30.9 %copy-start.5 = (s32[2,2]{1,0:T(2,128)S(1)}, s32[2,2]{1,0:T(2,128)}, u32[]{:S(2)}) copy-start(s32[2,2]{1,0:T(2,128)} %align_ref) | copy-start | bytes 52
  26.5 21.8 %collective-permute-start.5 = (bf16[5,128,256]{2,1,0:T(8,128)(2,1)S(1)}, bf16[5,128,256]{2,1,0:T(8,128)(2,1)S(1)}, u32[]{:S(2)}, u32[]{:S(2)}) collective-permute-start(bf16[5,128,256]{2,1,0:T(8,128)(2,1)S(1)} %pack_tokens.1.pair_ref.p0), channel_id=1, source_target_pairs={{0,252},{4,0},{8,4},{12,8},{16,12},{20,16},{24,20},{28,24},{32,28}... | collective-permute-start | bytes 983048 | tf_op jit(solution)/shard_map/ppermute | solution.py:27
  40.6 21.4 %collective-permute-start.9 = (bf16[5,128,256]{2,1,0:T(8,128)(2,1)S(1)}, bf16[5,128,256]{2,1,0:T(8,128)(2,1)S(1)}, u32[]{:S(2)}, u32[]{:S(2)}) collective-permute-start(bf16[5,128,256]{2,1,0:T(8,128)(2,1)S(1)} %pack_tokens.1.pair_ref.p0), channel_id=1, source_target_pairs={{0,4},{4,8},{8,12},{12,16},{16,20},{20,24},{24,28},{28,32},{32,36}... | collective-permute-start | bytes 983048 | tf_op jit(solution)/shard_map/ppermute | solution.py:27
  48.3 12.7 %collective-permute-start.6 = (f32[16,256]{1,0:T(8,128)S(1)}, f32[16,256]{1,0:T(8,128)S(1)}, u32[]{:S(2)}, u32[]{:S(2)}) collective-permute-start(f32[16,256]{1,0:T(8,128)S(1)} %get-tuple-element.33.stats_ref.s0), channel_id=1, source_target_pairs={{0,4},{4,8},{8,12},{12,16},{16,20},{20,24},{24,28},{28,32},{32,36}... | collective-permute-start | bytes 49160 | tf_op jit(solution)/shard_map/ppermute | solution.py:27
  48.4 23.9 %collective-permute-start.10 = (bf16[5,128,256]{2,1,0:T(8,128)(2,1)S(1)}, bf16[5,128,256]{2,1,0:T(8,128)(2,1)S(1)}, u32[]{:S(2)}, u32[]{:S(2)}) collective-permute-start(bf16[5,128,256]{2,1,0:T(8,128)(2,1)S(1)} %pack_tokens.1.pair_ref.p0), channel_id=1, source_target_pairs={{0,8},{4,12},{8,16},{12,20},{16,24},{20,28},{24,32},{28,36},{32,40... | collective-permute-start | bytes 983048 | tf_op jit(solution)/shard_map/ppermute | solution.py:27
  54.2 18.0 %collective-permute-start.11 = (f32[16,256]{1,0:T(8,128)S(1)}, f32[16,256]{1,0:T(8,128)S(1)}, u32[]{:S(2)}, u32[]{:S(2)}) collective-permute-start(f32[16,256]{1,0:T(8,128)S(1)} %get-tuple-element.33.stats_ref.s0), channel_id=1, source_target_pairs={{0,252},{4,0},{8,4},{12,8},{16,12},{20,16},{24,20},{28,24},{32,28}... | collective-permute-start | bytes 49160 | tf_op jit(solution)/shard_map/ppermute | solution.py:27
  54.2 18.0 %collective-permute-start.12 = (f32[16,256]{1,0:T(8,128)S(1)}, f32[16,256]{1,0:T(8,128)S(1)}, u32[]{:S(2)}, u32[]{:S(2)}) collective-permute-start(f32[16,256]{1,0:T(8,128)S(1)} %get-tuple-element.33.stats_ref.s0), channel_id=1, source_target_pairs={{0,8},{4,12},{8,16},{12,20},{16,24},{20,28},{24,32},{28,36},{32,40... | collective-permute-start | bytes 49160 | tf_op jit(solution)/shard_map/ppermute | solution.py:27
  61.6 6.6 %collective-permute-start.7 = (bf16[2,320,256]{2,1,0:T(8,128)(2,1)S(1)}, bf16[2,320,256]{2,1,0:T(8,128)(2,1)S(1)}, u32[]{:S(2)}, u32[]{:S(2)}) collective-permute-start(bf16[2,320,256]{2,1,0:T(8,128)(2,1)S(1)} %get-tuple-element.30), channel_id=1, source_target_pairs={{0,2},{1,3},{2,0},{3,1},{4,6},{5,7},{6,4},{7,5},{8,10},{9,11},{10,... | collective-permute-start | bytes 983048 | tf_op jit(solution)/shard_map/ppermute | solution.py:274
  68.3 9.5 %collective-permute-start.8 = (bf16[320,256]{1,0:T(8,128)(2,1)S(1)}, bf16[320,256]{1,0:T(8,128)(2,1)S(1)}, u32[]{:S(2)}, u32[]{:S(2)}) collective-permute-start(bf16[320,256]{1,0:T(8,128)(2,1)S(1)} %fusion.3), channel_id=1, source_target_pairs={{0,1},{1,0},{2,3},{3,2},{4,5},{5,4},{6,7},{7,6},{8,9},{9,8},{10,11... | collective-permute-start | bytes 491528 | tf_op jit(solution)/shard_map/ppermute | solution.py:274

commit v4 on v3

--- a/solution.py
+++ b/solution.py
@@ -18,7 +18,6 @@
 NN = (((1,), (0,)), ((), ()))
 VMEM = pl.BlockSpec(memory_space=pltpu.VMEM)
 SMEM = pl.BlockSpec(memory_space=pltpu.SMEM)
-HBM = pl.BlockSpec(memory_space=pltpu.HBM)
 PARAMS = pltpu.CompilerParams(vmem_limit_bytes=20 * 1024 * 1024)
 
 
@@ -33,19 +32,6 @@
 
 def iota(shape, dim):
     return lax.broadcasted_iota(jnp.int32, shape, dim)
-
-
-def pack_frames(keys_ref, values_ref, out_ref, done):
-    copies = []
-    for head in range(out_ref.shape[0]):
-        rows = pl.ds(head * DH, DH)
-        for side, source in enumerate((keys_ref, values_ref)):
-            target = out_ref.at[head, pl.ds(side * DH, DH)]
-            copies.append(pltpu.make_async_copy(source.at[rows], target, done.at[side, head]))
-    for copy in copies:
-        copy.start()
-    for copy in copies:
-        copy.wait()
 
 
 def pack_tokens(me_ref, own_ref, far_ref, other_ref, weight_ref, queries_ref, out_ref, whole):
@@ -285,13 +271,8 @@
     shape = jax.ShapeDtypeStruct
 
     grad_far = flipped(grad_out, 2)
-    frame_pack = call(
-        pack_frames,
-        shape((heads, PAIR, frames), bf16),
-        [HBM] * 2,
-        keys,
-        values,
-        scratch=[pltpu.SemaphoreType.DMA((2, heads))],
+    frame_pack = jnp.concatenate(
+        [keys.reshape(heads, DH, frames), values.reshape(heads, DH, frames)], axis=1
     )
     grad_own = after(grad_out, frame_pack)
     grad_other = flipped(jnp.concatenate([grad_own, grad_far], axis=0), 1)

time: 78.7 us -> 76.4 us (0.971)
  local copies, waits for them, and re-layouts: 2.62 us -> 0.67 us
  other arithmetic: 0.8 us -> 2 us
  Pallas kernels: 19.1 us -> 18.1 us
    ppermute x9, waiting for transfers between devices: 28.6 us -> 26.6 us  [ring(): lax.ppermute(value, 'seq', [(i, (i + by) % count) for i in range(count)])]
    unnamed x12 -> x8, local copies, waits for them, and re-layouts: 1.96 us -> 0.02 us
    ppermute x4, waiting for transfers between devices: 2.29 us -> 3.99 us  [flipped(): lax.ppermute(value, 'mp', [(i, i ^ by) for i in range(lax.axis_size('mp'))])]
    concatenate x0 -> x1, other arithmetic: none -> 1.2 us  [on_device(): jnp.concatenate([keys.reshape(heads, DH, frames), values.reshape(heads, D...]
    pallas_call x6 -> x5, Pallas kernels: 19.1 us -> 18.1 us  [call(): pl.pallas_call(kernel, out_shape=outs, in_specs=specs, out_specs=(VMEM,)...]
  transfers between devices with their start and end apart: 13 -> 13, of which waited for: 4 -> 4; matrix products, arithmetic and copies ran while one was open for 1% -> 3% of each run, Pallas kernels for 24% -> 24%
where the time goes in v4:
time: 76.4 us; the launch traced here: 76.3 us
  waiting for transfers between devices  30.5 us (40%)
  starting transfers between devices  24.2 us (32%)
  Pallas kernels  18.1 us (24%)
  other arithmetic  2 us (3%)
    ppermute x9, waiting for transfers between devices, ring(): lax.ppermute(value, 'seq', [(i, (i + by) % count) for i in range(count)])  26.6 us
    pallas_call x5, Pallas kernels, call(): pl.pallas_call(kernel, out_shape=outs, in_specs=specs, out_specs=(VMEM,)...  18.1 us
    ppermute x9, starting transfers between devices, ring(): lax.ppermute(value, 'seq', [(i, (i + by) % count) for i in range(count)])  16.4 us
    ppermute x4, starting transfers between devices, flipped(): lax.ppermute(value, 'mp', [(i, i ^ by) for i in range(lax.axis_size('mp'))])  7.77 us
    ppermute x4, waiting for transfers between devices, flipped(): lax.ppermute(value, 'mp', [(i, i ^ by) for i in range(lax.axis_size('mp'))])  3.99 us
  transfers between devices with their start and end apart: 13, of which 4 were waited for; matrix products, arithmetic and copies ran while one was open for 3% of the time, Pallas kernels for 24%

profile of v4, /device:TPU:113, one launch (start us, length us, event | category | flops | bytes accessed | tf_op | source)
XLA Modules:
  0.0 76.3 jit_solution(12014270460808048098)
XLA Ops:
  0.6 1.3 %collective-permute-start = (bf16[320,256]{1,0:T(8,128)(2,1)}, bf16[320,256]{1,0:T(8,128)(2,1)S(1)}, u32[]{:S(2)}, u32[]{:S(2)}) collective-permute-start(bf16[320,256]{1,0:T(8,128)(2,1)} %bitcast.27), channel_id=1, source_target_pairs={{0,2},{1,3},{2,0},{3,1},{4,6},{5,7},{6,4},{7,5},{8,10},{9,11},{10,... | collective-permute-start | bytes 491528 | tf_op jit(solution)/shard_map/ppermute | solution.py:260
  1.9 1.2 %pad_maximum_fusion.f1.own_ref = bf16[5,128,512]{2,1,0:T(8,128)(2,1)S(1)} fusion(bf16[5,64,512]{2,1,0:T(8,128)(2,1)} %bitcast.31, bf16[5,64,512]{2,1,0:T(8,128)(2,1)} %bitcast.32), kind=kLoop, calls=%fused_computation | loop fusion | flops 1310720 | bytes 1310720 | tf_op jit(solution)/shard_map/concatenate | solution.py:274
  3.1 0.1 collective-permute-start.4
  3.3 2.7 %collective-permute-done.far_ref = bf16[320,256]{1,0:T(8,128)(2,1)S(1)} collective-permute-done((bf16[320,256]{1,0:T(8,128)(2,1)}, bf16[320,256]{1,0:T(8,128)(2,1)S(1)}, u32[]{:S(2)}, u32[]{:S(2)}) %collective-permute-start) | collective-permute-done | bytes 163872 | tf_op jit(solution)/shard_map/ppermute | solution.py:260
  6.0 1.0 %collective-permute-start.2 = (bf16[5,128,512]{2,1,0:T(8,128)(2,1)S(1)}, bf16[5,128,512]{2,1,0:T(8,128)(2,1)}, u32[]{:S(2)}, u32[]{:S(2)}) collective-permute-start(bf16[5,128,512]{2,1,0:T(8,128)(2,1)S(1)} %pad_maximum_fusion.f1.own_ref), channel_id=1, source_target_pairs={{0,4},{4,8},{8,12},{12,16},{16,20},{20,24},{24,28},{28,32},{32,36}... | collective-permute-start | bytes 1966088 | tf_op jit(solution)/shard_map/ppermute | solution.py:26
  7.0 0.5 collective-permute-start.3
  7.5 2.2 %collective-permute-start.1 = (bf16[640,256]{1,0:T(8,128)(2,1)S(1)}, bf16[640,256]{1,0:T(8,128)(2,1)S(1)}, u32[]{:S(2)}, u32[]{:S(2)}) collective-permute-start(bf16[640,256]{1,0:T(8,128)(2,1)S(1)} %pad_maximum_fusion.1), channel_id=1, source_target_pairs={{0,1},{1,0},{2,3},{3,2},{4,5},{5,4},{6,7},{7,6},{8,9},{9,8},{10,11... | collective-permute-start | bytes 983048 | tf_op jit(solution)/shard_map/ppermute | solution.py:260
  9.7 1.3 %collective-permute-done.1.other_ref = bf16[640,256]{1,0:T(8,128)(2,1)S(1)} collective-permute-done((bf16[640,256]{1,0:T(8,128)(2,1)S(1)}, bf16[640,256]{1,0:T(8,128)(2,1)S(1)}, u32[]{:S(2)}, u32[]{:S(2)}) %collective-permute-start.1) | collective-permute-done | bytes 327712 | tf_op jit(solution)/shard_map/ppermute | solution.py:260
  11.0 0.4 pack_tokens.1.pair_ref.p0
  11.4 0.0 copy-start.3
  11.4 0.6 copy.10
  12.0 12.5 %collective-permute-done.4.f3 = bf16[5,128,512]{2,1,0:T(8,128)(2,1)S(1)} collective-permute-done((bf16[5,128,512]{2,1,0:T(8,128)(2,1)S(1)}, bf16[5,128,512]{2,1,0:T(8,128)(2,1)S(1)}, u32[]{:S(2)}, u32[]{:S(2)}) %collective-permute-start.4) | collective-permute-done | bytes 655392 | tf_op jit(solution)/shard_map/ppermute | solution.py:26
  24.5 0.0 collective-permute-start.5
  24.5 14.0 %collective-permute-done.2.f0 = bf16[5,128,512]{2,1,0:T(8,128)(2,1)} collective-permute-done((bf16[5,128,512]{2,1,0:T(8,128)(2,1)S(1)}, bf16[5,128,512]{2,1,0:T(8,128)(2,1)}, u32[]{:S(2)}, u32[]{:S(2)}) %collective-permute-start.2) | collective-permute-done | bytes 655392 | tf_op jit(solution)/shard_map/ppermute | solution.py:26
  38.6 0.0 collective-permute-done.3.f2
  38.6 2.3 %collective-permute-start.9 = (bf16[5,128,256]{2,1,0:T(8,128)(2,1)S(1)}, bf16[5,128,256]{2,1,0:T(8,128)(2,1)S(1)}, u32[]{:S(2)}, u32[]{:S(2)}) collective-permute-start(bf16[5,128,256]{2,1,0:T(8,128)(2,1)S(1)} %pack_tokens.1.pair_ref.p0), channel_id=1, source_target_pairs={{0,4},{4,8},{8,12},{12,16},{16,20},{20,24},{24,28},{28,32},{32,36}... | collective-permute-start | bytes 983048 | tf_op jit(solution)/shard_map/ppermute | solution.py:26
  40.9 5.4 %forward.1 = (bf16[320,256]{1,0:T(8,128)(2,1)S(1)}, f32[16,256]{1,0:T(8,128)S(1)}) custom-call(s32[1]{0:T(128)} %bitcast.8.place_ref, s32[2,2]{1,0:T(2,128)S(1)} %copy-done.3, bf16[5,128,256]{2,1,0:T(8,128)(2,1)S(1)} %pack_tokens.1.pair_ref.p0, bf16[5,128,512]{2,1,0:T(8,128)(2,1)} %collective-permute-done.2.f0, ...), custom_call_target="tpu_custom_call" | custom-call | flops 4000000000 | tf_op jit(solution)/shard_map/forward/pallas_call | solution.py:248
  46.3 0.0 collective-permute-done.5.p2
  46.3 0.1 collective-permute-start.6
  46.4 5.6 %collective-permute-start.10 = (bf16[5,128,256]{2,1,0:T(8,128)(2,1)S(1)}, bf16[5,128,256]{2,1,0:T(8,128)(2,1)S(1)}, u32[]{:S(2)}, u32[]{:S(2)}) collective-permute-start(bf16[5,128,256]{2,1,0:T(8,128)(2,1)S(1)} %pack_tokens.1.pair_ref.p0), channel_id=1, source_target_pairs={{0,8},{4,12},{8,16},{12,20},{16,24},{20,28},{24,32},{28,36},{32,40... | collective-permute-start | bytes 983048 | tf_op jit(solution)/shard_map/ppermute | solution.py:26
  52.0 0.0 collective-permute-start.11
  52.0 6.8 %collective-permute-start.12 = (f32[16,256]{1,0:T(8,128)S(1)}, f32[16,256]{1,0:T(8,128)S(1)}, u32[]{:S(2)}, u32[]{:S(2)}) collective-permute-start(f32[16,256]{1,0:T(8,128)S(1)} %get-tuple-element.33.stats_ref.s0), channel_id=1, source_target_pairs={{0,8},{4,12},{8,16},{12,20},{16,24},{20,28},{24,32},{28,36},{32,40... | collective-permute-start | bytes 49160 | tf_op jit(solution)/shard_map/ppermute | solution.py:26
  58.8 0.0 collective-permute-done.6.s1
  58.9 0.6 project.1
  59.4 0.1 collective-permute-start.7
  59.5 6.2 %query_side.1 = bf16[320,256]{1,0:T(8,128)(2,1)} custom-call(s32[1]{0:T(128)} %bitcast.8.place_ref, bf16[5,128,256]{2,1,0:T(8,128)(2,1)S(1)} %pack_tokens.1.pair_ref.p0, f32[16,256]{1,0:T(8,128)S(1)} %get-tuple-element.33.stats_ref.s0, bf16[5,128,512]{2,1,0:T(8,128)(2,1)} %collective-permute-done.2.f0, bf16[5,128,512]{2,1,0:T(8,128)(2,1)S(1)} %pad_maximum_fusion.f1.own_ref, ...), custom_call_target="tpu_custom_call" | custom-call | flops 4000000000 | tf_op jit(solution)/shard_map/query_side/pallas_call | solution.py:248
  65.8 0.0 collective-permute-done.7
  65.8 0.1 convert_add_fusion
  65.9 4.2 %collective-permute-start.8 = (bf16[320,256]{1,0:T(8,128)(2,1)S(1)}, bf16[320,256]{1,0:T(8,128)(2,1)S(1)}, u32[]{:S(2)}, u32[]{:S(2)}) collective-permute-start(bf16[320,256]{1,0:T(8,128)(2,1)S(1)} %fusion.3), channel_id=1, source_target_pairs={{0,1},{1,0},{2,3},{3,2},{4,5},{5,4},{6,7},{7,6},{8,9},{9,8},{10,11... | collective-permute-start | bytes 491528 | tf_op jit(solution)/shard_map/ppermute | solution.py:260
  70.0 0.0 collective-permute-done.11.s2
  70.1 5.5 %frame_side.1 = (bf16[320,512]{1,0:T(8,128)(2,1)}, bf16[320,512]{1,0:T(8,128)(2,1)}) custom-call(s32[1]{0:T(128)} %bitcast.8.place_ref, bf16[5,128,512]{2,1,0:T(8,128)(2,1)S(1)} %pad_maximum_fusion.f1.own_ref, bf16[5,128,256]{2,1,0:T(8,128)(2,1)S(1)} %pack_tokens.1.pair_ref.p0, bf16[5,128,256]{2,1,0:T(8,128)(2,1)S(1)} %collective-permute-done.9.p1, ...), custom_call_target="tpu_custom_call" | custom-call | flops 4000000000 | tf_op jit(solution)/shard_map/frame_side/pallas_call | solution.py:248
  75.6 0.7 fusion.2
  (13 shorter events, 0.1 us)
Async XLA Ops:
  0.6 6.8 %copy-start.1 = (bf16[256,320]{0,1:T(8,128)(2,1)S(1)}, bf16[256,320]{0,1:T(8,128)(2,1)}, u32[]{:S(2)}) copy-start(bf16[256,320]{0,1:T(8,128)(2,1)} %param.10) | copy-start | bytes 491524
  0.6 5.4 %collective-permute-start = (bf16[320,256]{1,0:T(8,128)(2,1)}, bf16[320,256]{1,0:T(8,128)(2,1)S(1)}, u32[]{:S(2)}, u32[]{:S(2)}) collective-permute-start(bf16[320,256]{1,0:T(8,128)(2,1)} %bitcast.27), channel_id=1, source_target_pairs={{0,2},{1,3},{2,0},{3,1},{4,6},{5,7},{6,4},{7,5},{8,10},{9,11},{10,... | collective-permute-start | bytes 491528 | tf_op jit(solution)/shard_map/ppermute | solution.py:260
  1.9 9.0 %copy-start = (bf16[320,1280]{1,0:T(8,128)(2,1)S(1)}, bf16[320,1280]{1,0:T(8,128)(2,1)}, u32[]{:S(2)}) copy-start(bf16[320,1280]{1,0:T(8,128)(2,1)} %weight_ref.1) | copy-start | bytes 2457604
  1.9 9.0 %copy-start.2 = (bf16[256,320]{0,1:T(8,128)(2,1)S(1)}, bf16[256,320]{0,1:T(8,128)(2,1)}, u32[]{:S(2)}) copy-start(bf16[256,320]{0,1:T(8,128)(2,1)} %param.6) | copy-start | bytes 491524
  3.1 21.4 %collective-permute-start.4 = (bf16[5,128,512]{2,1,0:T(8,128)(2,1)S(1)}, bf16[5,128,512]{2,1,0:T(8,128)(2,1)S(1)}, u32[]{:S(2)}, u32[]{:S(2)}) collective-permute-start(bf16[5,128,512]{2,1,0:T(8,128)(2,1)S(1)} %pad_maximum_fusion.f1.own_ref), channel_id=1, source_target_pairs={{0,248},{4,252},{8,0},{12,4},{16,8},{20,12},{24,16},{28,20},{32,24... | collective-permute-start | bytes 1966088 | tf_op jit(solution)/shard_map/ppermute | solution.py:26
  6.0 32.6 %collective-permute-start.2 = (bf16[5,128,512]{2,1,0:T(8,128)(2,1)S(1)}, bf16[5,128,512]{2,1,0:T(8,128)(2,1)}, u32[]{:S(2)}, u32[]{:S(2)}) collective-permute-start(bf16[5,128,512]{2,1,0:T(8,128)(2,1)S(1)} %pad_maximum_fusion.f1.own_ref), channel_id=1, source_target_pairs={{0,4},{4,8},{8,12},{12,16},{16,20},{20,24},{24,28},{28,32},{32,36}... | collective-permute-start | bytes 1966088 | tf_op jit(solution)/shard_map/ppermute | solution.py:26
  7.0 31.6 %collective-permute-start.3 = (bf16[5,128,512]{2,1,0:T(8,128)(2,1)S(1)}, bf16[5,128,512]{2,1,0:T(8,128)(2,1)}, u32[]{:S(2)}, u32[]{:S(2)}) collective-permute-start(bf16[5,128,512]{2,1,0:T(8,128)(2,1)S(1)} %pad_maximum_fusion.f1.own_ref), channel_id=1, source_target_pairs={{0,252},{4,0},{8,4},{12,8},{16,12},{20,16},{24,20},{28,24},{32,28}... | collective-permute-start | bytes 1966088 | tf_op jit(solution)/shard_map/ppermute | solution.py:26
  7.5 3.4 %collective-permute-start.1 = (bf16[640,256]{1,0:T(8,128)(2,1)S(1)}, bf16[640,256]{1,0:T(8,128)(2,1)S(1)}, u32[]{:S(2)}, u32[]{:S(2)}) collective-permute-start(bf16[640,256]{1,0:T(8,128)(2,1)S(1)} %pad_maximum_fusion.1), channel_id=1, source_target_pairs={{0,1},{1,0},{2,3},{3,2},{4,5},{5,4},{6,7},{7,6},{8,9},{9,8},{10,11... | collective-permute-start | bytes 983048 | tf_op jit(solution)/shard_map/ppermute | solution.py:260
  11.4 29.5 %copy-start.3 = (s32[2,2]{1,0:T(2,128)S(1)}, s32[2,2]{1,0:T(2,128)}, u32[]{:S(2)}) copy-start(s32[2,2]{1,0:T(2,128)} %align_ref) | copy-start | bytes 52
  24.5 21.8 %collective-permute-start.5 = (bf16[5,128,256]{2,1,0:T(8,128)(2,1)S(1)}, bf16[5,128,256]{2,1,0:T(8,128)(2,1)S(1)}, u32[]{:S(2)}, u32[]{:S(2)}) collective-permute-start(bf16[5,128,256]{2,1,0:T(8,128)(2,1)S(1)} %pack_tokens.1.pair_ref.p0), channel_id=1, source_target_pairs={{0,252},{4,0},{8,4},{12,8},{16,12},{20,16},{24,20},{28,24},{32,28}... | collective-permute-start | bytes 983048 | tf_op jit(solution)/shard_map/ppermute | solution.py:26
  38.6 20.9 %collective-permute-start.9 = (bf16[5,128,256]{2,1,0:T(8,128)(2,1)S(1)}, bf16[5,128,256]{2,1,0:T(8,128)(2,1)S(1)}, u32[]{:S(2)}, u32[]{:S(2)}) collective-permute-start(bf16[5,128,256]{2,1,0:T(8,128)(2,1)S(1)} %pack_tokens.1.pair_ref.p0), channel_id=1, source_target_pairs={{0,4},{4,8},{8,12},{12,16},{16,20},{20,24},{24,28},{28,32},{32,36}... | collective-permute-start | bytes 983048 | tf_op jit(solution)/shard_map/ppermute | solution.py:26
  46.3 12.5 %collective-permute-start.6 = (f32[16,256]{1,0:T(8,128)S(1)}, f32[16,256]{1,0:T(8,128)S(1)}, u32[]{:S(2)}, u32[]{:S(2)}) collective-permute-start(f32[16,256]{1,0:T(8,128)S(1)} %get-tuple-element.33.stats_ref.s0), channel_id=1, source_target_pairs={{0,4},{4,8},{8,12},{12,16},{16,20},{20,24},{24,28},{28,32},{32,36}... | collective-permute-start | bytes 49160 | tf_op jit(solution)/shard_map/ppermute | solution.py:26
  46.4 23.7 %collective-permute-start.10 = (bf16[5,128,256]{2,1,0:T(8,128)(2,1)S(1)}, bf16[5,128,256]{2,1,0:T(8,128)(2,1)S(1)}, u32[]{:S(2)}, u32[]{:S(2)}) collective-permute-start(bf16[5,128,256]{2,1,0:T(8,128)(2,1)S(1)} %pack_tokens.1.pair_ref.p0), channel_id=1, source_target_pairs={{0,8},{4,12},{8,16},{12,20},{16,24},{20,28},{24,32},{28,36},{32,40... | collective-permute-start | bytes 983048 | tf_op jit(solution)/shard_map/ppermute | solution.py:26
  52.0 18.0 %collective-permute-start.11 = (f32[16,256]{1,0:T(8,128)S(1)}, f32[16,256]{1,0:T(8,128)S(1)}, u32[]{:S(2)}, u32[]{:S(2)}) collective-permute-start(f32[16,256]{1,0:T(8,128)S(1)} %get-tuple-element.33.stats_ref.s0), channel_id=1, source_target_pairs={{0,252},{4,0},{8,4},{12,8},{16,12},{20,16},{24,20},{28,24},{32,28}... | collective-permute-start | bytes 49160 | tf_op jit(solution)/shard_map/ppermute | solution.py:26
  52.0 18.0 %collective-permute-start.12 = (f32[16,256]{1,0:T(8,128)S(1)}, f32[16,256]{1,0:T(8,128)S(1)}, u32[]{:S(2)}, u32[]{:S(2)}) collective-permute-start(f32[16,256]{1,0:T(8,128)S(1)} %get-tuple-element.33.stats_ref.s0), channel_id=1, source_target_pairs={{0,8},{4,12},{8,16},{12,20},{16,24},{20,28},{24,32},{28,36},{32,40... | collective-permute-start | bytes 49160 | tf_op jit(solution)/shard_map/ppermute | solution.py:26
  59.4 6.3 %collective-permute-start.7 = (bf16[2,320,256]{2,1,0:T(8,128)(2,1)S(1)}, bf16[2,320,256]{2,1,0:T(8,128)(2,1)S(1)}, u32[]{:S(2)}, u32[]{:S(2)}) collective-permute-start(bf16[2,320,256]{2,1,0:T(8,128)(2,1)S(1)} %get-tuple-element.30), channel_id=1, source_target_pairs={{0,2},{1,3},{2,0},{3,1},{4,6},{5,7},{6,4},{7,5},{8,10},{9,11},{10,... | collective-permute-start | bytes 983048 | tf_op jit(solution)/shard_map/ppermute | solution.py:260
  65.9 9.7 %collective-permute-start.8 = (bf16[320,256]{1,0:T(8,128)(2,1)S(1)}, bf16[320,256]{1,0:T(8,128)(2,1)S(1)}, u32[]{:S(2)}, u32[]{:S(2)}) collective-permute-start(bf16[320,256]{1,0:T(8,128)(2,1)S(1)} %fusion.3), channel_id=1, source_target_pairs={{0,1},{1,0},{2,3},{3,2},{4,5},{5,4},{6,7},{7,6},{8,9},{9,8},{10,11... | collective-permute-start | bytes 491528 | tf_op jit(solution)/shard_map/ppermute | solution.py:260

commit v5 on v4

--- a/solution.py
+++ b/solution.py
@@ -294,7 +294,7 @@
     turned_weight = after(out_weight, token_pack).T
     sent_pack = after(token_pack, window[3])
     late_pack = after(token_pack, *window)
-    token_packs = [ring(late_pack, 1), ring(sent_pack, -1), ring(late_pack, 2)]
+    token_packs = [ring(late_pack, 1), ring(sent_pack, -1), None]
 
     attended, stats = call(
         forward,
@@ -308,6 +308,7 @@
         steps=1,
     )
     sent_stats = after(stats, token_packs[1])
+    token_packs[2] = ring(after(token_pack, sent_stats), 2)
     near_stats = [ring(sent_stats, 1), ring(sent_stats, -1), ring(sent_stats, 2)]
 
     kept, sent = call(

time: 76.4 us -> 76.4 us (level)
  the two profiles are of different devices: /device:TPU:113 before, /device:TPU:2 now
where the time goes in v5:
time: 76.4 us; the launch traced here: 76.3 us
  starting transfers between devices  33.4 us (44%)
  waiting for transfers between devices  21.3 us (28%)
  Pallas kernels  18.2 us (24%)
  other arithmetic  2 us (3%)
    ppermute x9, starting transfers between devices, ring(): lax.ppermute(value, 'seq', [(i, (i + by) % count) for i in range(count)])  29 us
    ppermute x9, waiting for transfers between devices, ring(): lax.ppermute(value, 'seq', [(i, (i + by) % count) for i in range(count)])  19.7 us
    pallas_call x5, Pallas kernels, call(): pl.pallas_call(kernel, out_shape=outs, in_specs=specs, out_specs=(VMEM,)...  18.2 us
    ppermute x4, starting transfers between devices, flipped(): lax.ppermute(value, 'mp', [(i, i ^ by) for i in range(lax.axis_size('mp'))])  4.42 us
    ppermute x4, waiting for transfers between devices, flipped(): lax.ppermute(value, 'mp', [(i, i ^ by) for i in range(lax.axis_size('mp'))])  1.62 us
  transfers between devices with their start and end apart: 13, of which 6 were waited for; matrix products, arithmetic and copies ran while one was open for 3% of the time, Pallas kernels for 24%

profile of v5, /device:TPU:2, one launch (start us, length us, event | category | flops | bytes accessed | tf_op | source)
XLA Modules:
  0.0 76.3 jit_solution(5902209452952031090)
XLA Ops:
  0.6 2.4 %collective-permute-start = (bf16[320,256]{1,0:T(8,128)(2,1)}, bf16[320,256]{1,0:T(8,128)(2,1)S(1)}, u32[]{:S(2)}, u32[]{:S(2)}) collective-permute-start(bf16[320,256]{1,0:T(8,128)(2,1)} %bitcast.27), channel_id=1, source_target_pairs={{0,2},{1,3},{2,0},{3,1},{4,6},{5,7},{6,4},{7,5},{8,10},{9,11},{10,... | collective-permute-start | bytes 491528 | tf_op jit(solution)/shard_map/ppermute | solution.py:260
  3.0 1.2 %pad_maximum_fusion.f1.own_ref = bf16[5,128,512]{2,1,0:T(8,128)(2,1)S(1)} fusion(bf16[5,64,512]{2,1,0:T(8,128)(2,1)} %bitcast.31, bf16[5,64,512]{2,1,0:T(8,128)(2,1)} %bitcast.32), kind=kLoop, calls=%fused_computation | loop fusion | flops 1310720 | bytes 1310720 | tf_op jit(solution)/shard_map/concatenate | solution.py:274
  4.2 8.7 %collective-permute-start.4 = (bf16[5,128,512]{2,1,0:T(8,128)(2,1)S(1)}, bf16[5,128,512]{2,1,0:T(8,128)(2,1)S(1)}, u32[]{:S(2)}, u32[]{:S(2)}) collective-permute-start(bf16[5,128,512]{2,1,0:T(8,128)(2,1)S(1)} %pad_maximum_fusion.f1.own_ref), channel_id=1, source_target_pairs={{0,248},{4,252},{8,0},{12,4},{16,8},{20,12},{24,16},{28,20},{32,24... | collective-permute-start | bytes 1966088 | tf_op jit(solution)/shard_map/ppermute | solution.py:26
  12.9 0.0 collective-permute-done.far_ref
  12.9 3.9 %collective-permute-start.3 = (bf16[5,128,512]{2,1,0:T(8,128)(2,1)S(1)}, bf16[5,128,512]{2,1,0:T(8,128)(2,1)}, u32[]{:S(2)}, u32[]{:S(2)}) collective-permute-start(bf16[5,128,512]{2,1,0:T(8,128)(2,1)S(1)} %pad_maximum_fusion.f1.own_ref), channel_id=1, source_target_pairs={{0,252},{4,0},{8,4},{12,8},{16,12},{20,16},{24,20},{28,24},{32,28}... | collective-permute-start | bytes 1966088 | tf_op jit(solution)/shard_map/ppermute | solution.py:26
  16.7 0.0 collective-permute-start.2
  16.8 0.1 collective-permute-start.1
  16.9 1.6 %collective-permute-done.1.other_ref = bf16[640,256]{1,0:T(8,128)(2,1)S(1)} collective-permute-done((bf16[640,256]{1,0:T(8,128)(2,1)S(1)}, bf16[640,256]{1,0:T(8,128)(2,1)S(1)}, u32[]{:S(2)}, u32[]{:S(2)}) %collective-permute-start.1) | collective-permute-done | bytes 327712 | tf_op jit(solution)/shard_map/ppermute | solution.py:260
  18.5 0.4 pack_tokens.1.pair_ref.p0
  18.9 0.0 copy-start.3
  18.9 0.6 copy.10
  19.6 8.5 %collective-permute-done.4.f3 = bf16[5,128,512]{2,1,0:T(8,128)(2,1)S(1)} collective-permute-done((bf16[5,128,512]{2,1,0:T(8,128)(2,1)S(1)}, bf16[5,128,512]{2,1,0:T(8,128)(2,1)S(1)}, u32[]{:S(2)}, u32[]{:S(2)}) %collective-permute-start.4) | collective-permute-done | bytes 655392 | tf_op jit(solution)/shard_map/ppermute | solution.py:26
  28.1 7.8 %collective-permute-start.5 = (bf16[5,128,256]{2,1,0:T(8,128)(2,1)S(1)}, bf16[5,128,256]{2,1,0:T(8,128)(2,1)S(1)}, u32[]{:S(2)}, u32[]{:S(2)}) collective-permute-start(bf16[5,128,256]{2,1,0:T(8,128)(2,1)S(1)} %pack_tokens.1.pair_ref.p0), channel_id=1, source_target_pairs={{0,252},{4,0},{8,4},{12,8},{16,12},{20,16},{24,20},{28,24},{32,28}... | collective-permute-start | bytes 983048 | tf_op jit(solution)/shard_map/ppermute | solution.py:26
  35.9 6.3 %collective-permute-done.3.f2 = bf16[5,128,512]{2,1,0:T(8,128)(2,1)} collective-permute-done((bf16[5,128,512]{2,1,0:T(8,128)(2,1)S(1)}, bf16[5,128,512]{2,1,0:T(8,128)(2,1)}, u32[]{:S(2)}, u32[]{:S(2)}) %collective-permute-start.3) | collective-permute-done | bytes 655392 | tf_op jit(solution)/shard_map/ppermute | solution.py:26
  42.2 0.0 collective-permute-done.2.f0
  42.2 5.4 %forward.1 = (bf16[320,256]{1,0:T(8,128)(2,1)S(1)}, f32[16,256]{1,0:T(8,128)S(1)}) custom-call(s32[1]{0:T(128)} %bitcast.8.place_ref, s32[2,2]{1,0:T(2,128)S(1)} %copy-done.3, bf16[5,128,256]{2,1,0:T(8,128)(2,1)S(1)} %pack_tokens.1.pair_ref.p0, bf16[5,128,512]{2,1,0:T(8,128)(2,1)} %collective-permute-done.2.f0, ...), custom_call_target="tpu_custom_call" | custom-call | flops 4000000000 | tf_op jit(solution)/shard_map/forward/pallas_call | solution.py:248
  47.6 0.1 collective-permute-done.5.p2
  47.7 0.0 collective-permute-start.6
  47.7 0.0 collective-permute-start.12
  47.8 8.6 %collective-permute-start.11 = (f32[16,256]{1,0:T(8,128)S(1)}, f32[16,256]{1,0:T(8,128)S(1)}, u32[]{:S(2)}, u32[]{:S(2)}) collective-permute-start(f32[16,256]{1,0:T(8,128)S(1)} %get-tuple-element.35.stats_ref.s0), channel_id=1, source_target_pairs={{0,252},{4,0},{8,4},{12,8},{16,12},{20,16},{24,20},{28,24},{32,28}... | collective-permute-start | bytes 49160 | tf_op jit(solution)/shard_map/ppermute | solution.py:26
  56.3 0.0 collective-permute-start.10
  56.3 1.8 %collective-permute-done.6.s1 = f32[16,256]{1,0:T(8,128)S(1)} collective-permute-done((f32[16,256]{1,0:T(8,128)S(1)}, f32[16,256]{1,0:T(8,128)S(1)}, u32[]{:S(2)}, u32[]{:S(2)}) %collective-permute-start.6) | collective-permute-done | bytes 16416 | tf_op jit(solution)/shard_map/ppermute | solution.py:26
  58.1 0.6 project.1
  58.7 1.9 %collective-permute-start.7 = (bf16[2,320,256]{2,1,0:T(8,128)(2,1)S(1)}, bf16[2,320,256]{2,1,0:T(8,128)(2,1)S(1)}, u32[]{:S(2)}, u32[]{:S(2)}) collective-permute-start(bf16[2,320,256]{2,1,0:T(8,128)(2,1)S(1)} %get-tuple-element.31), channel_id=1, source_target_pairs={{0,2},{1,3},{2,0},{3,1},{4,6},{5,7},{6,4},{7,5},{8,10},{9,11},{10,... | collective-permute-start | bytes 983048 | tf_op jit(solution)/shard_map/ppermute | solution.py:260
  60.6 0.0 collective-permute-done.9.p1
  60.6 6.2 %query_side.1 = bf16[320,256]{1,0:T(8,128)(2,1)} custom-call(s32[1]{0:T(128)} %bitcast.8.place_ref, bf16[5,128,256]{2,1,0:T(8,128)(2,1)S(1)} %pack_tokens.1.pair_ref.p0, f32[16,256]{1,0:T(8,128)S(1)} %get-tuple-element.35.stats_ref.s0, bf16[5,128,512]{2,1,0:T(8,128)(2,1)} %collective-permute-done.2.f0, bf16[5,128,512]{2,1,0:T(8,128)(2,1)S(1)} %pad_maximum_fusion.f1.own_ref, ...), custom_call_target="tpu_custom_call" | custom-call | flops 4000000000 | tf_op jit(solution)/shard_map/query_side/pallas_call | solution.py:248
  66.8 0.0 collective-permute-done.7
  66.8 0.1 convert_add_fusion
  66.9 0.1 collective-permute-start.8
  67.0 3.0 %collective-permute-done.10.p3 = bf16[5,128,256]{2,1,0:T(8,128)(2,1)S(1)} collective-permute-done((bf16[5,128,256]{2,1,0:T(8,128)(2,1)S(1)}, bf16[5,128,256]{2,1,0:T(8,128)(2,1)S(1)}, u32[]{:S(2)}, u32[]{:S(2)}) %collective-permute-start.10) | collective-permute-done | bytes 327712 | tf_op jit(solution)/shard_map/ppermute | solution.py:26
  70.0 5.5 %frame_side.1 = (bf16[320,512]{1,0:T(8,128)(2,1)}, bf16[320,512]{1,0:T(8,128)(2,1)}) custom-call(s32[1]{0:T(128)} %bitcast.8.place_ref, bf16[5,128,512]{2,1,0:T(8,128)(2,1)S(1)} %pad_maximum_fusion.f1.own_ref, bf16[5,128,256]{2,1,0:T(8,128)(2,1)S(1)} %pack_tokens.1.pair_ref.p0, bf16[5,128,256]{2,1,0:T(8,128)(2,1)S(1)} %collective-permute-done.9.p1, ...), custom_call_target="tpu_custom_call" | custom-call | flops 4000000000 | tf_op jit(solution)/shard_map/frame_side/pallas_call | solution.py:248
  75.6 0.7 fusion.2
  (13 shorter events, 0.1 us)
Async XLA Ops:
  0.6 16.1 %copy-start.1 = (bf16[256,320]{0,1:T(8,128)(2,1)S(1)}, bf16[256,320]{0,1:T(8,128)(2,1)}, u32[]{:S(2)}) copy-start(bf16[256,320]{0,1:T(8,128)(2,1)} %param.10) | copy-start | bytes 491524
  0.6 12.2 %collective-permute-start = (bf16[320,256]{1,0:T(8,128)(2,1)}, bf16[320,256]{1,0:T(8,128)(2,1)S(1)}, u32[]{:S(2)}, u32[]{:S(2)}) collective-permute-start(bf16[320,256]{1,0:T(8,128)(2,1)} %bitcast.27), channel_id=1, source_target_pairs={{0,2},{1,3},{2,0},{3,1},{4,6},{5,7},{6,4},{7,5},{8,10},{9,11},{10,... | collective-permute-start | bytes 491528 | tf_op jit(solution)/shard_map/ppermute | solution.py:260
  3.0 15.5 %copy-start = (bf16[320,1280]{1,0:T(8,128)(2,1)S(1)}, bf16[320,1280]{1,0:T(8,128)(2,1)}, u32[]{:S(2)}) copy-start(bf16[320,1280]{1,0:T(8,128)(2,1)} %weight_ref.1) | copy-start | bytes 2457604
  3.0 15.5 %copy-start.2 = (bf16[256,320]{0,1:T(8,128)(2,1)S(1)}, bf16[256,320]{0,1:T(8,128)(2,1)}, u32[]{:S(2)}) copy-start(bf16[256,320]{0,1:T(8,128)(2,1)} %param.6) | copy-start | bytes 491524
  4.2 23.9 %collective-permute-start.4 = (bf16[5,128,512]{2,1,0:T(8,128)(2,1)S(1)}, bf16[5,128,512]{2,1,0:T(8,128)(2,1)S(1)}, u32[]{:S(2)}, u32[]{:S(2)}) collective-permute-start(bf16[5,128,512]{2,1,0:T(8,128)(2,1)S(1)} %pad_maximum_fusion.f1.own_ref), channel_id=1, source_target_pairs={{0,248},{4,252},{8,0},{12,4},{16,8},{20,12},{24,16},{28,20},{32,24... | collective-permute-start | bytes 1966088 | tf_op jit(solution)/shard_map/ppermute | solution.py:26
  12.9 29.3 %collective-permute-start.3 = (bf16[5,128,512]{2,1,0:T(8,128)(2,1)S(1)}, bf16[5,128,512]{2,1,0:T(8,128)(2,1)}, u32[]{:S(2)}, u32[]{:S(2)}) collective-permute-start(bf16[5,128,512]{2,1,0:T(8,128)(2,1)S(1)} %pad_maximum_fusion.f1.own_ref), channel_id=1, source_target_pairs={{0,252},{4,0},{8,4},{12,8},{16,12},{20,16},{24,20},{28,24},{32,28}... | collective-permute-start | bytes 1966088 | tf_op jit(solution)/shard_map/ppermute | solution.py:26
  16.7 25.4 %collective-permute-start.2 = (bf16[5,128,512]{2,1,0:T(8,128)(2,1)S(1)}, bf16[5,128,512]{2,1,0:T(8,128)(2,1)}, u32[]{:S(2)}, u32[]{:S(2)}) collective-permute-start(bf16[5,128,512]{2,1,0:T(8,128)(2,1)S(1)} %pad_maximum_fusion.f1.own_ref), channel_id=1, source_target_pairs={{0,4},{4,8},{8,12},{12,16},{16,20},{20,24},{24,28},{28,32},{32,36}... | collective-permute-start | bytes 1966088 | tf_op jit(solution)/shard_map/ppermute | solution.py:26
  16.8 1.7 %collective-permute-start.1 = (bf16[640,256]{1,0:T(8,128)(2,1)S(1)}, bf16[640,256]{1,0:T(8,128)(2,1)S(1)}, u32[]{:S(2)}, u32[]{:S(2)}) collective-permute-start(bf16[640,256]{1,0:T(8,128)(2,1)S(1)} %pad_maximum_fusion.1), channel_id=1, source_target_pairs={{0,1},{1,0},{2,3},{3,2},{4,5},{5,4},{6,7},{7,6},{8,9},{9,8},{10,11... | collective-permute-start | bytes 983048 | tf_op jit(solution)/shard_map/ppermute | solution.py:260
  18.9 23.2 %copy-start.3 = (s32[2,2]{1,0:T(2,128)S(1)}, s32[2,2]{1,0:T(2,128)}, u32[]{:S(2)}) copy-start(s32[2,2]{1,0:T(2,128)} %align_ref) | copy-start | bytes 52
  28.1 19.6 %collective-permute-start.5 = (bf16[5,128,256]{2,1,0:T(8,128)(2,1)S(1)}, bf16[5,128,256]{2,1,0:T(8,128)(2,1)S(1)}, u32[]{:S(2)}, u32[]{:S(2)}) collective-permute-start(bf16[5,128,256]{2,1,0:T(8,128)(2,1)S(1)} %pack_tokens.1.pair_ref.p0), channel_id=1, source_target_pairs={{0,252},{4,0},{8,4},{12,8},{16,12},{20,16},{24,20},{28,24},{32,28}... | collective-permute-start | bytes 983048 | tf_op jit(solution)/shard_map/ppermute | solution.py:26
  42.2 18.4 %collective-permute-start.9 = (bf16[5,128,256]{2,1,0:T(8,128)(2,1)S(1)}, bf16[5,128,256]{2,1,0:T(8,128)(2,1)S(1)}, u32[]{:S(2)}, u32[]{:S(2)}) collective-permute-start(bf16[5,128,256]{2,1,0:T(8,128)(2,1)S(1)} %pack_tokens.1.pair_ref.p0), channel_id=1, source_target_pairs={{0,4},{4,8},{8,12},{12,16},{16,20},{20,24},{24,28},{28,32},{32,36}... | collective-permute-start | bytes 983048 | tf_op jit(solution)/shard_map/ppermute | solution.py:26
  47.7 10.4 %collective-permute-start.6 = (f32[16,256]{1,0:T(8,128)S(1)}, f32[16,256]{1,0:T(8,128)S(1)}, u32[]{:S(2)}, u32[]{:S(2)}) collective-permute-start(f32[16,256]{1,0:T(8,128)S(1)} %get-tuple-element.35.stats_ref.s0), channel_id=1, source_target_pairs={{0,4},{4,8},{8,12},{12,16},{16,20},{20,24},{24,28},{28,32},{32,36}... | collective-permute-start | bytes 49160 | tf_op jit(solution)/shard_map/ppermute | solution.py:26
  47.7 19.3 %collective-permute-start.12 = (f32[16,256]{1,0:T(8,128)S(1)}, f32[16,256]{1,0:T(8,128)S(1)}, u32[]{:S(2)}, u32[]{:S(2)}) collective-permute-start(f32[16,256]{1,0:T(8,128)S(1)} %get-tuple-element.35.stats_ref.s0), channel_id=1, source_target_pairs={{0,8},{4,12},{8,16},{12,20},{16,24},{20,28},{24,32},{28,36},{32,40... | collective-permute-start | bytes 49160 | tf_op jit(solution)/shard_map/ppermute | solution.py:26
  47.8 19.2 %collective-permute-start.11 = (f32[16,256]{1,0:T(8,128)S(1)}, f32[16,256]{1,0:T(8,128)S(1)}, u32[]{:S(2)}, u32[]{:S(2)}) collective-permute-start(f32[16,256]{1,0:T(8,128)S(1)} %get-tuple-element.35.stats_ref.s0), channel_id=1, source_target_pairs={{0,252},{4,0},{8,4},{12,8},{16,12},{20,16},{24,20},{28,24},{32,28}... | collective-permute-start | bytes 49160 | tf_op jit(solution)/shard_map/ppermute | solution.py:26
  56.3 13.7 %collective-permute-start.10 = (bf16[5,128,256]{2,1,0:T(8,128)(2,1)S(1)}, bf16[5,128,256]{2,1,0:T(8,128)(2,1)S(1)}, u32[]{:S(2)}, u32[]{:S(2)}) collective-permute-start(bf16[5,128,256]{2,1,0:T(8,128)(2,1)S(1)} %pack_tokens.1.pair_ref.p0), channel_id=1, source_target_pairs={{0,8},{4,12},{8,16},{12,20},{16,24},{20,28},{24,32},{28,36},{32,40... | collective-permute-start | bytes 983048 | tf_op jit(solution)/shard_map/ppermute | solution.py:26
  58.7 8.1 %collective-permute-start.7 = (bf16[2,320,256]{2,1,0:T(8,128)(2,1)S(1)}, bf16[2,320,256]{2,1,0:T(8,128)(2,1)S(1)}, u32[]{:S(2)}, u32[]{:S(2)}) collective-permute-start(bf16[2,320,256]{2,1,0:T(8,128)(2,1)S(1)} %get-tuple-element.31), channel_id=1, source_target_pairs={{0,2},{1,3},{2,0},{3,1},{4,6},{5,7},{6,4},{7,5},{8,10},{9,11},{10,... | collective-permute-start | bytes 983048 | tf_op jit(solution)/shard_map/ppermute | solution.py:260
  66.9 8.7 %collective-permute-start.8 = (bf16[320,256]{1,0:T(8,128)(2,1)S(1)}, bf16[320,256]{1,0:T(8,128)(2,1)S(1)}, u32[]{:S(2)}, u32[]{:S(2)}) collective-permute-start(bf16[320,256]{1,0:T(8,128)(2,1)S(1)} %fusion.3), channel_id=1, source_target_pairs={{0,1},{1,0},{2,3},{3,2},{4,5},{5,4},{6,7},{7,6},{8,9},{9,8},{10,11... | collective-permute-start | bytes 491528 | tf_op jit(solution)/shard_map/ppermute | solution.py:260
